TPU v7x, 512 devices: a whole 4x8x8 slice. The times are simulated.
512 devices in a mesh: slab: 16 (over z, core), tile: 32 (over x, y).
Axes of the slice: x: 4, y: 8, z: 8, core: 2. Of those that a mesh axis runs over, the one named last changes fastest.
Arguments:
- density: bfloat16 [262144, 512], P(('slab', 'tile')), may hold values from 0.049804688 to 4
- brick_color: float32 [3, 262144], P(None, ('slab', 'tile')), may hold values from 0.1 to 1
- brick_row: int32 [262144], P(('slab', 'tile')), may hold values from 0 to 31, as said below
- brick_col: int32 [262144], P(('slab', 'tile')), may hold values from 0 to 1023, as said below
- brick_steps: int32 [262144], P(('slab', 'tile')), may hold values from 1 to 8
- depth_flip: int32 [32, 1024], P(None, 'tile'), may hold values from 0 to 1
- w_in: bfloat16 [32, 4, 3, 3], replicated, may hold values from -1.5 to 1.5
- w_enc: bfloat16 [32, 32, 3, 3], replicated, may hold values from -0.5 to 0.5
- w_dec: bfloat16 [32, 32, 3, 3], replicated, may hold values from -0.5 to 0.5
- w_dec2: bfloat16 [32, 32, 3, 3], replicated, may hold values from -0.5 to 0.5
- w_out: bfloat16 [3, 32], replicated, may hold values from -1 to 1
Outputs:
- denoised: bfloat16 [3, 256, 8192], P(None, 'slab', 'tile')
Inputs may be any that keep to these rules, and one draw needn't show every extreme that they name: `brick_row`: within one slab no two bricks name the same screen tile. The bricks of one device name at most 32 tiles in any one column block (tile columns j * 32 to (j + 1) * 32 - 1); in every slab some column block gets exactly 32 bricks from every device of that slab. `brick_col`: see brick_row.
All inputs are finite; a program needn't handle non-finite values.
Results may differ from a plain program's by a relative error of at most 0.0086.
Values may be sent and summed in bfloat16 or wider, within the bound.
A program may use at most 64 MiB of HBM per device.

v0:
```python
import jax
import jax.numpy as jnp
from jax import lax
from jax.sharding import PartitionSpec as P

PH = 16
PW = 256


STEP = 0.03


def with_halo(block, sides, width):
    for axis, dim in sides:
        count = lax.axis_size(axis)
        forward = [(i, i + 1) for i in range(count - 1)]
        backward = [(target, source) for source, target in forward]
        low = lax.ppermute(
            lax.slice_in_dim(block, block.shape[dim] - width, None, axis=dim), axis, forward
        )
        high = lax.ppermute(lax.slice_in_dim(block, 0, width, axis=dim), axis, backward)
        block = jnp.concatenate([low, block, high], axis=dim)
    return block


def ray_march(density, brick_color, brick_steps):
    count = density.shape[0]
    sigmas = density.astype(jnp.float32).reshape(count, 8, 64)
    tint = jnp.transpose(brick_color)[:, :, None]
    trans = jnp.ones((count, 64), jnp.float32)
    light = jnp.zeros((count, 3, 64), jnp.float32)
    for depth_idx in range(8):
        sigma = sigmas[:, depth_idx, :]
        alive = (brick_steps > depth_idx)[:, None]
        opacity = jnp.where(alive, 1.0 - jnp.exp(-STEP * sigma), 0.0)
        light = light + (trans * opacity * sigma)[:, None, :] * tint
        trans = trans * (1.0 - opacity)
    joined = jnp.concatenate([light, (1.0 - trans)[:, None, :]], axis=1)
    return joined.reshape(count, 256).astype(jnp.bfloat16)


def convolve(field, kernel):
    return lax.conv_general_dilated(
        field[None],
        kernel,
        (1, 1),
        "VALID",
        dimension_numbers=("NCHW", "OIHW", "NCHW"),
        preferred_element_type=jnp.float32,
    )[0]


def feature_halo(field):
    return with_halo(field, (("slab", 1), ("tile", 2)), 1)


def shards(
    density,
    brick_color,
    brick_row,
    brick_col,
    brick_steps,
    depth_flip,
    w_in,
    w_enc,
    w_dec,
    w_dec2,
    w_out,
):
    n_tile = lax.axis_size("tile")
    n_slab = lax.axis_size("slab")
    slab_pos = lax.axis_index("slab")
    tile_cols = PW // 8
    owned = n_slab * PH * PW // 64
    capacity = owned // n_tile
    per_block = PH * PW // 64
    partials = ray_march(density, brick_color, brick_steps)
    owners = brick_col // tile_cols
    onehot = (owners[:, None] == jnp.arange(n_tile, dtype=jnp.int32)[None, :]).astype(jnp.int32)
    ranks = jnp.sum(jnp.cumsum(onehot, axis=0) * onehot, axis=1) - 1
    slot_ids = owners * capacity + ranks
    local_ids = brick_row * tile_cols + (brick_col - owners * tile_cols)
    outgoing = jnp.zeros((n_tile * capacity, 256), jnp.bfloat16).at[slot_ids].set(partials)
    targets = jnp.full((n_tile * capacity,), owned, jnp.int32).at[slot_ids].set(local_ids)
    arrived, arrived_ids = (
        lax.all_to_all(
            outgoing.reshape(n_tile, capacity, 256), "tile", split_axis=0, concat_axis=0, tiled=True
        ),
        lax.all_to_all(
            targets.reshape(n_tile, capacity), "tile", split_axis=0, concat_axis=0, tiled=True
        ),
    )
    canvas = (
        jnp.zeros((owned, 256), jnp.bfloat16)
        .at[arrived_ids.reshape(-1)]
        .set(arrived.reshape(-1, 256), mode="drop")
    )
    layers = lax.all_to_all(
        canvas.reshape(1, owned, 256), "slab", split_axis=1, concat_axis=0, tiled=True
    )
    flip_rows = lax.dynamic_slice_in_dim(depth_flip, slab_pos * (PH // 8), PH // 8, 0)
    flipped = (flip_rows.reshape(per_block) == 1)[:, None]

    def blend_layer(layer_idx, carry):
        light, trans = carry
        near = lax.dynamic_index_in_dim(layers, layer_idx, 0, keepdims=False)
        far = lax.dynamic_index_in_dim(layers, n_slab - 1 - layer_idx, 0, keepdims=False)
        piece = jnp.where(flipped, far, near).astype(jnp.float32)
        light = light + jnp.tile(trans, (1, 3)) * piece[:, :192]
        trans = trans * (1.0 - piece[:, 192:])
        return (light, trans)

    start_light = jnp.zeros((per_block, 192), jnp.float32)
    start_trans = jnp.ones((per_block, 64), jnp.float32)
    light, trans = lax.fori_loop(0, n_slab, blend_layer, (start_light, start_trans))
    tiles = jnp.concatenate([light, 1.0 - trans], axis=1).astype(jnp.bfloat16)
    composite = jnp.transpose(tiles.reshape(PH // 8, tile_cols, 4, 8, 8), (2, 0, 3, 1, 4)).reshape(
        4, PH, PW
    )
    wide_input = with_halo(composite, (("slab", 1), ("tile", 2)), 1)
    e_first = jax.nn.relu(convolve(wide_input, w_in)).astype(jnp.bfloat16)
    e_second = jax.nn.relu(convolve(feature_halo(e_first), w_enc)).astype(jnp.bfloat16)
    d_first = jax.nn.relu(convolve(feature_halo(e_second), w_dec)).astype(jnp.bfloat16)
    d_second = jax.nn.relu(
        convolve(feature_halo(d_first), w_dec2) + e_first.astype(jnp.float32)
    ).astype(jnp.bfloat16)
    projected = jnp.dot(
        w_out, d_second.reshape(d_second.shape[0], PH * PW), preferred_element_type=jnp.float32
    ).reshape(3, PH, PW)
    return (composite[:3].astype(jnp.float32) + projected).astype(jnp.bfloat16)


def solution(mesh):
    return jax.shard_map(
        shards,
        mesh=mesh,
        in_specs=(
            P(("slab", "tile"), None),
            P(None, ("slab", "tile")),
            P(("slab", "tile")),
            P(("slab", "tile")),
            P(("slab", "tile")),
            P(None, "tile"),
            P(),
            P(),
            P(),
            P(),
            P(),
        ),
        out_specs=P(None, "slab", "tile"),
        check_vma=False,
    )
```

profile of v0, /device:TPU:1, one launch (start us, length us, event | category | flops | bytes accessed | tf_op | source)
XLA Modules:
  0.0 189.5 jit_solution(14167530755171719809)
XLA Ops:
  2.3 2.4 %scatter_custom_fusion = s32[1024]{0:T(1024)S(1)} fusion(s32[512]{0:T(512)S(1)} %compare_select_fusion.1, s32[512]{0:T(512)S(1)} %get-tuple-element.190, s32[]{:T(128)} %constant.110.clone.1), kind=kCustom, calls=%fused_computation.104 | custom fusion | bytes 4100 | tf_op jit(solution)/shard_map/scatter | solution.py:84
  5.5 10.5 %all-to-all-start = ((s32[32,1,32]{2,1,0:T(1,128)}), s32[32,1,32]{2,1,0:T(1,128)S(1)}, u32[]{:S(2)}, u32[]{:S(2)}) async-start(s32[32,1,32]{2,1,0:T(1,128)} %all_to_all.18), calls=%async_computation | async-start | bytes 32768 | tf_op jit(solution)/shard_map/all_to_all | solution.py:89
  18.9 3.1 %scatter_custom_fusion.1 = bf16[1024,256]{1,0:T(8,128)(2,1)} fusion(s32[512]{0:T(512)S(1)} %compare_select_fusion.1, bf16[512,256]{1,0:T(8,128)(2,1)S(1)} %copy.96, bf16[]{:T(256)} %constant.109.clone.1), kind=kCustom, calls=%fused_computation.60 | custom fusion | bytes 524290 | tf_op jit(solution)/shard_map/scatter | solution.py:83
  24.5 6.8 %all-to-all-start.1 = ((bf16[32,32,256]{2,1,0:T(8,128)(2,1)}), bf16[32,32,256]{2,1,0:T(8,128)(2,1)S(1)}, u32[]{:S(2)}, u32[]{:S(2)}) async-start(bf16[32,32,256]{2,1,0:T(8,128)(2,1)} %bitcast.8), calls=%async_computation.1 | async-start | bytes 1048576 | tf_op jit(solution)/shard_map/all_to_all | solution.py:86
  32.6 12.4 %all-to-all-done.1 = bf16[32,32,256]{2,1,0:T(8,128)(2,1)S(1)} async-done(((bf16[32,32,256]{2,1,0:T(8,128)(2,1)}), bf16[32,32,256]{2,1,0:T(8,128)(2,1)S(1)}, u32[]{:S(2)}, u32[]{:S(2)}) %all-to-all-start.1) | async-done | bytes 524320 | tf_op jit(solution)/shard_map/all_to_all | solution.py:86
  45.1 5.2 %scatter_custom_fusion.2 = bf16[1024,256]{1,0:T(8,128)(2,1)S(1)} fusion(s32[1024]{0:T(1024)S(1)} %bitcast.158, bf16[1024,256]{1,0:T(8,128)(2,1)S(1)} %bitcast.152, bf16[]{:T(256)} %constant.109.clone.1), kind=kCustom, calls=%fused_computation.58 | custom fusion | bytes 524290 | tf_op jit(solution)/shard_map/scatter | solution.py:96
  51.7 4.0 %reduce.6 = bf16[1024,256]{1,0:T(8,128)(2,1)S(1)} reduce(bf16[1024,1,256]{2,1,0:T(2,128)(2,1)S(1)} %bitcast.145, bf16[]{:T(256)} %broadcast.526), dimensions={1}, to_apply=%bitcast.132.reduce_sub_computation | reduce | bytes 1048578
  56.5 14.8 %all-to-all-start.2 = ((bf16[16,2,8192]{2,1,0:T(2,128)(2,1)}), bf16[16,2,8192]{2,1,0:T(2,128)(2,1)S(1)}, u32[]{:S(2)}, u32[]{:S(2)}) async-start(bf16[16,2,8192]{2,1,0:T(2,128)(2,1)} %reshape.424), calls=%async_computation.2 | async-start | bytes 1048576 | tf_op jit(solution)/shard_map/all_to_all | solution.py:98
  72.2 16.5 %all-to-all-done.2 = bf16[16,2,8192]{2,1,0:T(2,128)(2,1)S(1)} async-done(((bf16[16,2,8192]{2,1,0:T(2,128)(2,1)}), bf16[16,2,8192]{2,1,0:T(2,128)(2,1)S(1)}, u32[]{:S(2)}, u32[]{:S(2)}) %all-to-all-start.2) | async-done | bytes 524320 | tf_op jit(solution)/shard_map/all_to_all | solution.py:98
  97.1 2.5 %collective-permute-done.1 = bf16[4,1,256]{2,1,0:T(2,128)(2,1)S(1)} collective-permute-done((bf16[4,1,256]{2,1,0:T(2,128)(2,1)S(1)}, bf16[4,1,256]{2,1,0:T(2,128)(2,1)S(1)}, u32[]{:S(2)}, u32[]{:S(2)}) %collective-permute-start.1) | collective-permute-done | bytes 2080 | tf_op jit(solution)/shard_map/ppermute | solution.py:21
  99.7 3.7 %collective-permute-start.2 = (bf16[4,18,1]{2,1,0:T(8,128)(2,1)S(1)}, bf16[4,18,1]{2,1,0:T(8,128)(2,1)S(1)}, u32[]{:S(2)}, u32[]{:S(2)}) collective-permute-start(bf16[4,18,1]{2,1,0:T(8,128)(2,1)S(1)} %get-tuple-element.204), channel_id=1, source_target_pairs={{0,1},{1,2},{2,3},{3,4},{4,5},{5,6},{6,7},{7,8},{8,9},{9,10},{10,1... | collective-permute-start | bytes 440 | tf_op jit(solution)/shard_map/ppermute | solution.py:18
  104.8 3.3 %collective-permute-done.3 = bf16[4,18,1]{2,1,0:T(8,128)(2,1)S(1)} collective-permute-done((bf16[4,18,1]{2,1,0:T(8,128)(2,1)S(1)}, bf16[4,18,1]{2,1,0:T(8,128)(2,1)S(1)}, u32[]{:S(2)}, u32[]{:S(2)}) %collective-permute-start.3) | collective-permute-done | bytes 176 | tf_op jit(solution)/shard_map/ppermute | solution.py:21
  114.1 3.4 %collective-permute-start.4 = (bf16[32,1,256]{2,0,1:T(8,128)(2,1)S(1)}, bf16[32,1,256]{2,0,1:T(8,128)(2,1)S(1)}, u32[]{:S(2)}, u32[]{:S(2)}) collective-permute-start(bf16[32,1,256]{2,0,1:T(8,128)(2,1)S(1)} %get-tuple-element.202), channel_id=1, source_target_pairs={{0,32},{32,64},{64,96},{96,128},{128,160},{160,192},{192,224},{224... | collective-permute-start | bytes 49160 | tf_op jit(solution)/shard_map/ppermute | solution.py:18
  119.4 3.1 %collective-permute-done.5 = bf16[32,1,256]{2,0,1:T(8,128)(2,1)S(1)} collective-permute-done((bf16[32,1,256]{2,0,1:T(8,128)(2,1)S(1)}, bf16[32,1,256]{2,0,1:T(8,128)(2,1)S(1)}, u32[]{:S(2)}, u32[]{:S(2)}) %collective-permute-start.5) | collective-permute-done | bytes 16416 | tf_op jit(solution)/shard_map/ppermute | solution.py:21
  126.9 4.1 %collective-permute-done.7 = bf16[32,18,1]{2,0,1:T(8,128)(2,1)S(1)} collective-permute-done((bf16[32,18,1]{2,0,1:T(8,128)(2,1)S(1)}, bf16[32,18,1]{2,0,1:T(8,128)(2,1)S(1)}, u32[]{:S(2)}, u32[]{:S(2)}) %collective-permute-start.7) | collective-permute-done | bytes 1184 | tf_op jit(solution)/shard_map/ppermute | solution.py:21
  137.4 4.2 %collective-permute-start.8 = (bf16[32,1,256]{2,0,1:T(8,128)(2,1)S(1)}, bf16[32,1,256]{2,0,1:T(8,128)(2,1)S(1)}, u32[]{:S(2)}, u32[]{:S(2)}) collective-permute-start(bf16[32,1,256]{2,0,1:T(8,128)(2,1)S(1)} %get-tuple-element.200), channel_id=1, source_target_pairs={{0,32},{32,64},{64,96},{96,128},{128,160},{160,192},{192,224},{224... | collective-permute-start | bytes 49160 | tf_op jit(solution)/shard_map/ppermute | solution.py:18
  143.5 3.1 %collective-permute-done.9 = bf16[32,1,256]{2,0,1:T(8,128)(2,1)S(1)} collective-permute-done((bf16[32,1,256]{2,0,1:T(8,128)(2,1)S(1)}, bf16[32,1,256]{2,0,1:T(8,128)(2,1)S(1)}, u32[]{:S(2)}, u32[]{:S(2)}) %collective-permute-start.9) | collective-permute-done | bytes 16416 | tf_op jit(solution)/shard_map/ppermute | solution.py:21
  146.8 2.9 %collective-permute-start.10 = (bf16[32,18,1]{2,0,1:T(8,128)(2,1)S(1)}, bf16[32,18,1]{2,0,1:T(8,128)(2,1)S(1)}, u32[]{:S(2)}, u32[]{:S(2)}) collective-permute-start(bf16[32,18,1]{2,0,1:T(8,128)(2,1)S(1)} %get-tuple-element.194), channel_id=1, source_target_pairs={{0,1},{1,2},{2,3},{3,4},{4,5},{5,6},{6,7},{7,8},{8,9},{9,10},{10,1... | collective-permute-start | bytes 3464 | tf_op jit(solution)/shard_map/ppermute | solution.py:18
  151.8 4.1 %collective-permute-done.11 = bf16[32,18,1]{2,0,1:T(8,128)(2,1)S(1)} collective-permute-done((bf16[32,18,1]{2,0,1:T(8,128)(2,1)S(1)}, bf16[32,18,1]{2,0,1:T(8,128)(2,1)S(1)}, u32[]{:S(2)}, u32[]{:S(2)}) %collective-permute-start.11) | collective-permute-done | bytes 1184 | tf_op jit(solution)/shard_map/ppermute | solution.py:21
  162.4 4.2 %collective-permute-start.12 = (bf16[32,1,256]{2,0,1:T(8,128)(2,1)S(1)}, bf16[32,1,256]{2,0,1:T(8,128)(2,1)S(1)}, u32[]{:S(2)}, u32[]{:S(2)}) collective-permute-start(bf16[32,1,256]{2,0,1:T(8,128)(2,1)S(1)} %get-tuple-element.198), channel_id=1, source_target_pairs={{0,32},{32,64},{64,96},{96,128},{128,160},{160,192},{192,224},{224... | collective-permute-start | bytes 49160 | tf_op jit(solution)/shard_map/ppermute | solution.py:18
  168.6 3.1 %collective-permute-done.13 = bf16[32,1,256]{2,0,1:T(8,128)(2,1)S(1)} collective-permute-done((bf16[32,1,256]{2,0,1:T(8,128)(2,1)S(1)}, bf16[32,1,256]{2,0,1:T(8,128)(2,1)S(1)}, u32[]{:S(2)}, u32[]{:S(2)}) %collective-permute-start.13) | collective-permute-done | bytes 16416 | tf_op jit(solution)/shard_map/ppermute | solution.py:21
  171.8 3.2 %collective-permute-start.14 = (bf16[32,18,1]{2,0,1:T(8,128)(2,1)S(1)}, bf16[32,18,1]{2,0,1:T(8,128)(2,1)S(1)}, u32[]{:S(2)}, u32[]{:S(2)}) collective-permute-start(bf16[32,18,1]{2,0,1:T(8,128)(2,1)S(1)} %get-tuple-element.192), channel_id=1, source_target_pairs={{0,1},{1,2},{2,3},{3,4},{4,5},{5,6},{6,7},{7,8},{8,9},{9,10},{10,1... | collective-permute-start | bytes 3464 | tf_op jit(solution)/shard_map/ppermute | solution.py:18
  177.9 3.3 %collective-permute-done.15 = bf16[32,18,1]{2,0,1:T(8,128)(2,1)S(1)} collective-permute-done((bf16[32,18,1]{2,0,1:T(8,128)(2,1)S(1)}, bf16[32,18,1]{2,0,1:T(8,128)(2,1)S(1)}, u32[]{:S(2)}, u32[]{:S(2)}) %collective-permute-start.15) | collective-permute-done | bytes 1184 | tf_op jit(solution)/shard_map/ppermute | solution.py:21
  184.0 2.7 %select_add_fusion = bf16[16,8,33,32]{3,1,2,0:T(8,128)(2,1)S(1)} fusion(bf16[16,8,33,32]{3,1,2,0:T(8,128)(2,1)S(1)} %copy-done.2, bf16[32,32,3,3]{1,0,3,2:T(8,128)(2,1)} %param.22, bf16[32,18,1,7,2]{0,3,4,1,2:T(8,128)(2,1)S(1)} %slice.173, bf16[32,18,1,8,33]{0,3,4,1,2:T(8,128)(2,1)S(1)} %copy.113, pred[8,33]{0,1:T(8,128)(4,1)} %constant.140), kind=kOutput, calls=%fused_computation.14 | convolution fusion | flops 79365120 | bytes 879624 | tf_op jit(solution)/shard_map/conv_general_dilated | solution.py:43
  (177 shorter events, 62.9 us)
Async XLA Ops:
  0.0 133.7 %copy-start = (bf16[32,32,3,3]{1,0,3,2:T(8,128)(2,1)S(1)}, bf16[32,32,3,3]{1,0,3,2:T(8,128)(2,1)}, u32[]{:S(2)}) copy-start(bf16[32,32,3,3]{1,0,3,2:T(8,128)(2,1)} %param.20) | copy-start | bytes 55300
  5.5 19.1 %all-to-all-start = ((s32[32,1,32]{2,1,0:T(1,128)}), s32[32,1,32]{2,1,0:T(1,128)S(1)}, u32[]{:S(2)}, u32[]{:S(2)}) async-start(s32[32,1,32]{2,1,0:T(1,128)} %all_to_all.18), calls=%async_computation | async-start | bytes 32768 | tf_op jit(solution)/shard_map/all_to_all | solution.py:89
  24.5 20.5 %all-to-all-start.1 = ((bf16[32,32,256]{2,1,0:T(8,128)(2,1)}), bf16[32,32,256]{2,1,0:T(8,128)(2,1)S(1)}, u32[]{:S(2)}, u32[]{:S(2)}) async-start(bf16[32,32,256]{2,1,0:T(8,128)(2,1)} %bitcast.8), calls=%async_computation.1 | async-start | bytes 1048576 | tf_op jit(solution)/shard_map/all_to_all | solution.py:86
  56.5 32.2 %all-to-all-start.2 = ((bf16[16,2,8192]{2,1,0:T(2,128)(2,1)}), bf16[16,2,8192]{2,1,0:T(2,128)(2,1)S(1)}, u32[]{:S(2)}, u32[]{:S(2)}) async-start(bf16[16,2,8192]{2,1,0:T(2,128)(2,1)} %reshape.424), calls=%async_computation.2 | async-start | bytes 1048576 | tf_op jit(solution)/shard_map/all_to_all | solution.py:98
  92.0 17.0 %copy-start.7 = (bf16[32,4,3,3]{0,1,3,2:T(4,128)(2,1)S(1)}, bf16[32,4,3,3]{0,1,3,2:T(4,128)(2,1)}, u32[]{:S(2)}) copy-start(bf16[32,4,3,3]{0,1,3,2:T(4,128)(2,1)} %param.19) | copy-start | bytes 6916
  92.0 17.0 %copy-start.8 = (pred[8,33]{0,1:T(8,128)(4,1)S(1)}, pred[8,33]{0,1:T(8,128)(4,1)}, u32[]{:S(2)}) copy-start(pred[8,33]{0,1:T(8,128)(4,1)} %constant.140) | copy-start | bytes 796
  92.8 4.3 %collective-permute-start = (bf16[4,1,256]{2,1,0:T(2,128)(2,1)S(1)}, bf16[4,1,256]{2,1,0:T(2,128)(2,1)S(1)}, u32[]{:S(2)}, u32[]{:S(2)}) collective-permute-start(bf16[4,1,256]{2,1,0:T(2,128)(2,1)S(1)} %get-tuple-element.206), channel_id=1, source_target_pairs={{0,32},{32,64},{64,96},{96,128},{128,160},{160,192},{192,224},{224... | collective-permute-start | bytes 6152 | tf_op jit(solution)/shard_map/ppermute | solution.py:18
  94.7 4.9 %collective-permute-start.1 = (bf16[4,1,256]{2,1,0:T(2,128)(2,1)S(1)}, bf16[4,1,256]{2,1,0:T(2,128)(2,1)S(1)}, u32[]{:S(2)}, u32[]{:S(2)}) collective-permute-start(bf16[4,1,256]{2,1,0:T(2,128)(2,1)S(1)} %get-tuple-element.207), channel_id=1, source_target_pairs={{32,0},{64,32},{96,64},{128,96},{160,128},{192,160},{224,192},{256... | collective-permute-start | bytes 6152 | tf_op jit(solution)/shard_map/ppermute | solution.py:21
  99.7 5.0 %collective-permute-start.2 = (bf16[4,18,1]{2,1,0:T(8,128)(2,1)S(1)}, bf16[4,18,1]{2,1,0:T(8,128)(2,1)S(1)}, u32[]{:S(2)}, u32[]{:S(2)}) collective-permute-start(bf16[4,18,1]{2,1,0:T(8,128)(2,1)S(1)} %get-tuple-element.204), channel_id=1, source_target_pairs={{0,1},{1,2},{2,3},{3,4},{4,5},{5,6},{6,7},{7,8},{8,9},{9,10},{10,1... | collective-permute-start | bytes 440 | tf_op jit(solution)/shard_map/ppermute | solution.py:18
  103.5 4.6 %collective-permute-start.3 = (bf16[4,18,1]{2,1,0:T(8,128)(2,1)S(1)}, bf16[4,18,1]{2,1,0:T(8,128)(2,1)S(1)}, u32[]{:S(2)}, u32[]{:S(2)}) collective-permute-start(bf16[4,18,1]{2,1,0:T(8,128)(2,1)S(1)} %get-tuple-element.205), channel_id=1, source_target_pairs={{1,0},{2,1},{3,2},{4,3},{5,4},{6,5},{7,6},{8,7},{9,8},{10,9},{11,1... | collective-permute-start | bytes 440 | tf_op jit(solution)/shard_map/ppermute | solution.py:21
  114.1 5.3 %collective-permute-start.4 = (bf16[32,1,256]{2,0,1:T(8,128)(2,1)S(1)}, bf16[32,1,256]{2,0,1:T(8,128)(2,1)S(1)}, u32[]{:S(2)}, u32[]{:S(2)}) collective-permute-start(bf16[32,1,256]{2,0,1:T(8,128)(2,1)S(1)} %get-tuple-element.202), channel_id=1, source_target_pairs={{0,32},{32,64},{64,96},{96,128},{128,160},{160,192},{192,224},{224... | collective-permute-start | bytes 49160 | tf_op jit(solution)/shard_map/ppermute | solution.py:18
  117.4 5.1 %collective-permute-start.5 = (bf16[32,1,256]{2,0,1:T(8,128)(2,1)S(1)}, bf16[32,1,256]{2,0,1:T(8,128)(2,1)S(1)}, u32[]{:S(2)}, u32[]{:S(2)}) collective-permute-start(bf16[32,1,256]{2,0,1:T(8,128)(2,1)S(1)} %get-tuple-element.203), channel_id=1, source_target_pairs={{32,0},{64,32},{96,64},{128,96},{160,128},{192,160},{224,192},{256... | collective-permute-start | bytes 49160 | tf_op jit(solution)/shard_map/ppermute | solution.py:21
  122.7 4.2 %collective-permute-start.6 = (bf16[32,18,1]{2,0,1:T(8,128)(2,1)S(1)}, bf16[32,18,1]{2,0,1:T(8,128)(2,1)S(1)}, u32[]{:S(2)}, u32[]{:S(2)}) collective-permute-start(bf16[32,18,1]{2,0,1:T(8,128)(2,1)S(1)} %get-tuple-element.196), channel_id=1, source_target_pairs={{0,1},{1,2},{2,3},{3,4},{4,5},{5,6},{6,7},{7,8},{8,9},{9,10},{10,1... | collective-permute-start | bytes 3464 | tf_op jit(solution)/shard_map/ppermute | solution.py:18
  124.8 6.2 %collective-permute-start.7 = (bf16[32,18,1]{2,0,1:T(8,128)(2,1)S(1)}, bf16[32,18,1]{2,0,1:T(8,128)(2,1)S(1)}, u32[]{:S(2)}, u32[]{:S(2)}) collective-permute-start(bf16[32,18,1]{2,0,1:T(8,128)(2,1)S(1)} %get-tuple-element.197), channel_id=1, source_target_pairs={{1,0},{2,1},{3,2},{4,3},{5,4},{6,5},{7,6},{8,7},{9,8},{10,9},{11,1... | collective-permute-start | bytes 3464 | tf_op jit(solution)/shard_map/ppermute | solution.py:21
  137.4 6.1 %collective-permute-start.8 = (bf16[32,1,256]{2,0,1:T(8,128)(2,1)S(1)}, bf16[32,1,256]{2,0,1:T(8,128)(2,1)S(1)}, u32[]{:S(2)}, u32[]{:S(2)}) collective-permute-start(bf16[32,1,256]{2,0,1:T(8,128)(2,1)S(1)} %get-tuple-element.200), channel_id=1, source_target_pairs={{0,32},{32,64},{64,96},{96,128},{128,160},{160,192},{192,224},{224... | collective-permute-start | bytes 49160 | tf_op jit(solution)/shard_map/ppermute | solution.py:18
  141.6 5.1 %collective-permute-start.9 = (bf16[32,1,256]{2,0,1:T(8,128)(2,1)S(1)}, bf16[32,1,256]{2,0,1:T(8,128)(2,1)S(1)}, u32[]{:S(2)}, u32[]{:S(2)}) collective-permute-start(bf16[32,1,256]{2,0,1:T(8,128)(2,1)S(1)} %get-tuple-element.201), channel_id=1, source_target_pairs={{32,0},{64,32},{96,64},{128,96},{160,128},{192,160},{224,192},{256... | collective-permute-start | bytes 49160 | tf_op jit(solution)/shard_map/ppermute | solution.py:21
  146.8 5.0 %collective-permute-start.10 = (bf16[32,18,1]{2,0,1:T(8,128)(2,1)S(1)}, bf16[32,18,1]{2,0,1:T(8,128)(2,1)S(1)}, u32[]{:S(2)}, u32[]{:S(2)}) collective-permute-start(bf16[32,18,1]{2,0,1:T(8,128)(2,1)S(1)} %get-tuple-element.194), channel_id=1, source_target_pairs={{0,1},{1,2},{2,3},{3,4},{4,5},{5,6},{6,7},{7,8},{8,9},{9,10},{10,1... | collective-permute-start | bytes 3464 | tf_op jit(solution)/shard_map/ppermute | solution.py:18
  149.7 6.2 %collective-permute-start.11 = (bf16[32,18,1]{2,0,1:T(8,128)(2,1)S(1)}, bf16[32,18,1]{2,0,1:T(8,128)(2,1)S(1)}, u32[]{:S(2)}, u32[]{:S(2)}) collective-permute-start(bf16[32,18,1]{2,0,1:T(8,128)(2,1)S(1)} %get-tuple-element.195), channel_id=1, source_target_pairs={{1,0},{2,1},{3,2},{4,3},{5,4},{6,5},{7,6},{8,7},{9,8},{10,9},{11,1... | collective-permute-start | bytes 3464 | tf_op jit(solution)/shard_map/ppermute | solution.py:21
  157.3 1.4 copy-start.6
  162.4 6.2 %collective-permute-start.12 = (bf16[32,1,256]{2,0,1:T(8,128)(2,1)S(1)}, bf16[32,1,256]{2,0,1:T(8,128)(2,1)S(1)}, u32[]{:S(2)}, u32[]{:S(2)}) collective-permute-start(bf16[32,1,256]{2,0,1:T(8,128)(2,1)S(1)} %get-tuple-element.198), channel_id=1, source_target_pairs={{0,32},{32,64},{64,96},{96,128},{128,160},{160,192},{192,224},{224... | collective-permute-start | bytes 49160 | tf_op jit(solution)/shard_map/ppermute | solution.py:18
  166.6 5.1 %collective-permute-start.13 = (bf16[32,1,256]{2,0,1:T(8,128)(2,1)S(1)}, bf16[32,1,256]{2,0,1:T(8,128)(2,1)S(1)}, u32[]{:S(2)}, u32[]{:S(2)}) collective-permute-start(bf16[32,1,256]{2,0,1:T(8,128)(2,1)S(1)} %get-tuple-element.199), channel_id=1, source_target_pairs={{32,0},{64,32},{96,64},{128,96},{160,128},{192,160},{224,192},{256... | collective-permute-start | bytes 49160 | tf_op jit(solution)/shard_map/ppermute | solution.py:21
  171.8 6.1 %collective-permute-start.14 = (bf16[32,18,1]{2,0,1:T(8,128)(2,1)S(1)}, bf16[32,18,1]{2,0,1:T(8,128)(2,1)S(1)}, u32[]{:S(2)}, u32[]{:S(2)}) collective-permute-start(bf16[32,18,1]{2,0,1:T(8,128)(2,1)S(1)} %get-tuple-element.192), channel_id=1, source_target_pairs={{0,1},{1,2},{2,3},{3,4},{4,5},{5,6},{6,7},{7,8},{8,9},{9,10},{10,1... | collective-permute-start | bytes 3464 | tf_op jit(solution)/shard_map/ppermute | solution.py:18
  175.0 6.2 %collective-permute-start.15 = (bf16[32,18,1]{2,0,1:T(8,128)(2,1)S(1)}, bf16[32,18,1]{2,0,1:T(8,128)(2,1)S(1)}, u32[]{:S(2)}, u32[]{:S(2)}) collective-permute-start(bf16[32,18,1]{2,0,1:T(8,128)(2,1)S(1)} %get-tuple-element.193), channel_id=1, source_target_pairs={{1,0},{2,1},{3,2},{4,3},{5,4},{6,5},{7,6},{8,7},{9,8},{10,9},{11,1... | collective-permute-start | bytes 3464 | tf_op jit(solution)/shard_map/ppermute | solution.py:21
  182.6 1.4 copy-start.2
  (4 other events, 3.5 us)
where the time goes:
time: 193 us; the launch traced here: 190 us
  starting transfers between devices  71.6 us (37%)
  waiting for transfers between devices  59.5 us (31%)
  local copies, waits for them, and re-layouts  37 us (19%)
  other arithmetic  11.7 us (6%)
  matrix products  8.29 us (4%)
    ppermute x8, waiting for transfers between devices, with_halo(): lax.ppermute(lax.slice_in_dim(block, 0, width, axis=dim), axis, backward)  26.6 us
    ppermute x8, starting transfers between devices, with_halo(): lax.ppermute(lax.slice_in_dim(block, block.shape[dim] - width, None, axis...  25.6 us
    all_to_all x1, waiting for transfers between devices, shards(): lax.all_to_all(canvas.reshape(1, owned, 256), 'slab', split_axis=1, conca...  16.5 us
    all_to_all x1, starting transfers between devices, shards(): lax.all_to_all(canvas.reshape(1, owned, 256), 'slab', split_axis=1, conca...  14.8 us
    ppermute x8, starting transfers between devices, with_halo(): lax.ppermute(lax.slice_in_dim(block, 0, width, axis=dim), axis, backward)  13.8 us
    all_to_all x1, waiting for transfers between devices, shards(): lax.all_to_all(outgoing.reshape(n_tile, capacity, 256), 'tile', split_axi...  12.4 us
    all_to_all x1, starting transfers between devices, shards(): lax.all_to_all(targets.reshape(n_tile, capacity), 'tile', split_axis=0, c...  10.5 us
    conv_general_dilated x4, matrix products, convolve(): lax.conv_general_dilated(field[None], kernel, (1, 1), 'VALID', dimension_...  8.14 us
  transfers between devices with their start and end apart: 19, of which 13 were waited for; matrix products, arithmetic and copies ran while one was open for 5% of the time, Pallas kernels for 0%

commit v1 on v0

v1 whole, which is shorter than its diff:
```python
import functools
import jax
import jax.numpy as jnp
from jax import lax
from jax.experimental import pallas as pl
from jax.experimental.pallas import tpu as pltpu
from jax.sharding import PartitionSpec as P

MESH = pl.DeviceIdType.MESH
BF16 = jnp.bfloat16
F32 = jnp.float32
STEP = 0.03
CAP = 32
PITCH = 40
PAD = 8
LIGHT_TOP = 2.5
ALPHA_TOP = 0.625
LEVELS = 65535.0


def iota(shape, dim):
    return lax.broadcasted_iota(jnp.int32, shape, dim)


def as_bf16(cond):
    return jnp.where(cond, 1.0, 0.0).astype(BF16)


def mm(a, b):
    return jnp.dot(a, b, preferred_element_type=F32)


def mm_nt(a, b):
    return lax.dot_general(a, b, (((1,), (1,)), ((), ())), preferred_element_type=F32)


def mm_tn(a, b):
    return lax.dot_general(a, b, (((0,), (0,)), ((), ())), preferred_element_type=F32)


def scales(shape):
    front = iota(shape, 1) < 64
    return jnp.where(front, LIGHT_TOP / LEVELS, ALPHA_TOP / LEVELS)


def split(levels):
    high = levels // 256
    low = levels - 256 * high
    return jnp.concatenate([high.astype(F32), low.astype(F32)], axis=1).astype(BF16)


def join(halves):
    levels = (256.0 * halves[:, 0:128] + halves[:, 128:256]).astype(jnp.int32)
    return (levels - 32768).astype(jnp.int16)


def build_weights(w_in, w_layers, w_out, w1, wb, wo):
    spread = as_bf16(iota((32, 256), 0) == iota((32, 256), 1) % 32)
    lane_x = iota((32, 256), 1) // 32
    for layer, w_ref in enumerate(w_layers):
        turned = jnp.transpose(w_ref[...].astype(F32))
        for ky in range(3):
            taps = [
                mm(turned[:, 32 * (3 * ky + kx) : 32 * (3 * ky + kx) + 32].astype(BF16), spread)
                for kx in range(3)
            ]
            base = 256 * ky
            for x_in in range(8):
                total = jnp.zeros((32, 256), F32)
                for kx in range(3):
                    total = jnp.where(lane_x == x_in - kx + 1, taps[kx], total)
                wb[layer, base + 32 * x_in : base + 32 * x_in + 32, :] = total.astype(BF16)
            edge = 768 + 128 * ky
            wb[layer, edge : edge + 32, :] = jnp.where(lane_x == 7, taps[2], 0.0).astype(BF16)
            wb[layer, edge + 32 : edge + 96, :] = jnp.zeros((64, 256), BF16)
            wb[layer, edge + 96 : edge + 128, :] = jnp.where(lane_x == 0, taps[0], 0.0).astype(BF16)
    row = iota((128, 256), 0)
    lane_x = iota((128, 256), 1) // 32
    third = row // 32
    x_in = (row % 32) // 4 + jnp.where(third == 1, -8, jnp.where(third == 2, 8, 0))
    pick = as_bf16((iota((128, 4), 0) % 4 == iota((128, 4), 1)) & (iota((128, 4), 0) < 96))
    for ky in range(3):
        total = jnp.zeros((128, 256), F32)
        for kx in range(3):
            tap = mm(mm(pick, w_in[3 * ky + kx]).astype(BF16), spread)
            total = jnp.where(lane_x == x_in - kx + 1, tap, total)
        w1[128 * ky : 128 * ky + 128, :] = total.astype(BF16)
    spread_t = as_bf16(iota((256, 32), 1) == iota((256, 32), 0) % 32)
    same_x = iota((256, 256), 0) // 32 == iota((256, 256), 1) % 8
    row = iota((128, 256), 0)
    for c in range(3):
        along = mm_nt(spread_t, jnp.broadcast_to(w_out[c : c + 1, :], (256, 32)))
        wo[0:256, 256 * c : 256 * c + 256] = jnp.where(same_x, along, 0.0).astype(BF16)
        own = (row < 32) & (row % 4 == c) & (row // 4 == iota((128, 256), 1) % 8)
        wo[256:384, 256 * c : 256 * c + 256] = as_bf16(own)


def ray_march(density, steps, part):
    lane = iota((64, 128), 1)
    front = lane < 64
    half = jnp.where(front, 0, 1)
    for chunk in range(density.shape[0] // 64):
        rows = slice(64 * chunk, 64 * chunk + 64)
        group = steps[:, 128 * (64 * chunk // 128) : 128 * (64 * chunk // 128) + 128].astype(F32)
        off = (64 * chunk) % 128
        eye = iota((64, 128), 0) + off == iota((64, 128), 1)
        alive = mm(jnp.where(eye, group, 0.0).astype(BF16), jnp.ones((128, 128), BF16))
        alive = alive.astype(jnp.int32)
        light = jnp.zeros((64, 128), F32)
        trans = jnp.ones((64, 128), F32)
        for j in range(4):
            sigma = density[rows, 128 * j : 128 * j + 128].astype(F32)
            keep = jnp.where(half + 2 * j < alive, jnp.exp(-STEP * sigma), 1.0)
            emit = (1.0 - keep) * sigma
            other = pltpu.roll(keep, 64, 1)
            light = light + trans * jnp.where(front, 1.0, other) * emit
            trans = trans * (keep * other)
        light = light + pltpu.roll(light, 64, 1)
        value = jnp.where(
            front, light * (LEVELS / LIGHT_TOP), (1.0 - trans) * (LEVELS / ALPHA_TOP)
        )
        part[rows, :] = split((value + 0.5).astype(jnp.int32))


def kernel(
    n_slab,
    n_tile,
    density,
    color,
    brick_row,
    brick_col,
    steps,
    flip,
    w_in,
    w_enc,
    w_dec,
    w_dec2,
    w_out,
    out,
    part,
    place,
    canvas_of,
    a_out,
    a_in,
    am_out,
    am_in,
    canvas,
    b_out,
    b_in,
    bm_out,
    bm_in,
    tint,
    h_own,
    h_edge,
    h_rows,
    h_sides,
    ext,
    x0,
    x1,
    e1,
    e2,
    d1,
    edge,
    w1,
    wb,
    wo,
    am_send,
    am_recv,
    a_send,
    a_recv,
    bm_send,
    bm_recv,
    b_send,
    b_recv,
    h_send,
    h_recv,
):
    s = lax.axis_index("slab")
    t = lax.axis_index("tile")
    bricks = density.shape[0]
    slots = CAP * n_tile
    owned = 64 * n_slab

    def tile_peer(i):
        return (s, lax.rem(t + i, n_tile))

    def slab_peer(j):
        return (lax.rem(s + j, n_slab), t)

    def near(ds, dt):
        return (lax.rem(s + ds + n_slab, n_slab), lax.rem(t + dt + n_tile, n_tile))

    corners = [near(-1, -1), near(-1, 1), near(1, -1), near(1, 1)]
    greeted = (
        [tile_peer(i) for i in range(1, n_tile)]
        + [slab_peer(j) for j in range(1, n_slab)]
        + corners
    )
    barrier = pltpu.get_barrier_semaphore()
    for peer in greeted:
        pl.semaphore_signal(barrier, inc=1, device_id=peer, device_id_type=MESH)

    col = brick_col[...]
    row = brick_row[...]
    rel = (col // 32 - t + n_tile) % n_tile
    mine = iota((n_tile, bricks), 0) == rel
    before = as_bf16(iota((bricks, bricks), 0) < iota((bricks, bricks), 1))
    ahead = mm(as_bf16(mine), before)
    rank = jnp.sum(jnp.where(mine, ahead, 0.0), axis=0, keepdims=True).astype(jnp.int32)
    slot = rel * CAP + rank
    place[...] = as_bf16(iota((slots, bricks), 0) == slot)
    block = (row // 2 - s + n_slab) % n_slab
    tile_hi = (block * 2 + row % 2 + 1).astype(F32)
    tile_lo = (col % 32).astype(F32)
    tints = color[...]
    tints_hi = tints.astype(BF16).astype(F32)
    tints_lo = tints - tints_hi
    field = iota((16, bricks), 0)
    meta = jnp.zeros((16, bricks), F32)
    for c in range(3):
        meta = jnp.where(field == 2 * c, tints_hi[c : c + 1, :], meta)
        meta = jnp.where(field == 2 * c + 1, tints_lo[c : c + 1, :], meta)
    meta = jnp.where(field == 6, tile_hi, meta)
    meta = jnp.where(field == 7, tile_lo, meta)
    meta = jnp.where(field == 8, 1.0, meta)
    sent_meta = mm_nt(meta.astype(BF16), place[...]).astype(BF16)
    for g in range(slots // 128):
        am_out[g] = sent_meta[:, 128 * g : 128 * g + 128]
    am_in[0] = am_out[0]

    pl.semaphore_wait(barrier, len(greeted))

    def start(src, dst, send, recv, peer):
        copy = pltpu.make_async_remote_copy(
            src_ref=src,
            dst_ref=dst,
            send_sem=send,
            recv_sem=recv,
            device_id=peer,
            device_id_type=MESH,
        )
        copy.start()
        return copy

    am_copies = [
        start(am_out.at[i // 4], am_in.at[i], am_send.at[i], am_recv.at[i], tile_peer(i))
        for i in range(1, n_tile)
    ]

    ray_march(density, steps, part)
    a_copies = []
    for g in range(slots // 128):
        a_out[128 * g : 128 * g + 128, :] = join(
            mm(place[128 * g : 128 * g + 128, :], part[...])
        )
        for i in range(4 * g, 4 * g + 4):
            span = pl.ds(CAP * i, CAP)
            if i == 0:
                a_in[0:CAP, :] = a_out[0:CAP, :]
            else:
                a_copies.append(
                    start(
                        a_out.at[span], a_in.at[span], a_send.at[i], a_recv.at[i], tile_peer(i)
                    )
                )

    for copy in am_copies:
        copy.wait_recv()
    lane = iota((16, 128), 1)
    groups = []
    for g in range(slots // 128):
        got = am_in[4 * g].astype(F32)
        for q in range(1, 4):
            got = jnp.where(lane // 32 == q, am_in[4 * g + q].astype(F32), got)
        groups.append(got)
    arrived = jnp.concatenate(groups, axis=1)
    tile_id = (32.0 * arrived[6:7, :] + arrived[7:8, :] - 32.0).astype(jnp.int32)
    canvas_of[...] = as_bf16(iota((owned, slots), 0) == tile_id)
    tile_meta = mm_nt(arrived.astype(BF16), canvas_of[...]).astype(BF16)
    for g in range(n_slab // 2):
        bm_out[g] = tile_meta[:, 128 * g : 128 * g + 128]
    bm_in[0] = bm_out[0]
    bm_copies = [
        start(bm_out.at[j // 2], bm_in.at[j], bm_send.at[j], bm_recv.at[j], slab_peer(j))
        for j in range(1, n_slab)
    ]

    build_weights(w_in, (w_enc, w_dec, w_dec2), w_out, w1, wb, wo)
    ext[...] = jnp.zeros(ext.shape, F32)
    for ref in (x0, e1, e2, d1):
        width = ref.shape[1]
        ref[0:PAD, :] = jnp.zeros((PAD, width), F32)
        ref[ref.shape[0] - PAD :, :] = jnp.zeros((PAD, width), F32)

    chunk = min(256, slots)
    for k in range(slots // chunk):
        for i in range(max(1, k * chunk // CAP), (k + 1) * chunk // CAP):
            a_copies[i - 1].wait_recv()
        span = slice(k * chunk, (k + 1) * chunk)
        term = mm(canvas_of[:, span], split(a_in[span, :].astype(jnp.int32) + 32768))
        if k == 0:
            canvas[...] = term
        else:
            canvas[...] += term
    b_copies = []
    for j in range(n_slab):
        piece = join(canvas[64 * j : 64 * j + 64, :])
        if j == 0:
            b_in[0] = piece
        else:
            b_out[j] = piece
            b_copies.append(
                start(b_out.at[j], b_in.at[j], b_send.at[j], b_recv.at[j], slab_peer(j))
            )

    for copy in bm_copies:
        copy.wait_recv()
    lane_c = iota((16, 256), 1) // 64
    field = iota((16, 256), 0)
    choose = as_bf16(((field // 2 == lane_c) & (lane_c < 3) & (field < 6)) | ((field == 8) & (lane_c == 3)))
    for j in range(n_slab):
        both = mm_tn(bm_in[j], choose)
        tint[j] = both[64 * (j % 2) : 64 * (j % 2) + 64, :]

    flips = flip[pl.ds(2 * s, 2), :]
    same = iota((32, 32), 0) == iota((32, 32), 1)
    flipped = (
        jnp.concatenate(
            [
                jnp.sum(jnp.where(same, flips[r : r + 1, :], 0), axis=1, keepdims=True)
                for r in range(2)
            ],
            axis=0,
        )
        == 1
    )

    for copy in b_copies:
        copy.wait_recv()
    front = iota((64, 128), 1) < 64
    scale = scales((64, 128))
    light0 = jnp.zeros((64, 128), F32)
    light1 = jnp.zeros((64, 128), F32)
    trans = jnp.ones((64, 128), F32)
    for k in range(n_slab):
        first = lax.rem(s - k + n_slab, n_slab)
        last = lax.rem(s - (n_slab - 1 - k) + n_slab, n_slab)
        level = jnp.where(
            flipped, b_in[last].astype(jnp.int32), b_in[first].astype(jnp.int32)
        )
        piece = (level + 32768).astype(F32) * scale
        hue = jnp.where(flipped, tint[last], tint[first])
        turned = pltpu.roll(piece, 64, 1)
        part0 = (jnp.where(front, piece, turned) * hue[:, 0:128]).astype(BF16).astype(F32)
        part1 = (piece * hue[:, 128:256]).astype(BF16).astype(F32)
        alpha = jnp.where(front, pltpu.roll(part1, 64, 1), part1)
        light0 = light0 + trans * part0
        light1 = light1 + trans * part1
        trans = trans * (1.0 - alpha)
    composite = jnp.concatenate([light0, light1], axis=1).astype(BF16)
    h_own[...] = composite
    own = composite.astype(F32)
    edge_row = iota((16, 256), 0)
    for side, at in ((0, 0), (1, 31)):
        h_edge[side] = jnp.where(
            edge_row == 0,
            own[at : at + 1, :],
            jnp.where(edge_row == 1, own[at + 32 : at + 33, :], 0.0),
        ).astype(BF16)
    up, down, left, right = near(-1, 0), near(1, 0), near(0, -1), near(0, 1)
    plan = [
        (h_own.at[pl.ds(0, 32)], h_rows.at[1], up),
        (h_own.at[pl.ds(32, 32)], h_rows.at[0], down),
        (h_edge.at[0], h_sides.at[1], left),
        (h_edge.at[1], h_sides.at[0], right),
        (h_edge.at[0], h_sides.at[5], corners[0]),
        (h_edge.at[1], h_sides.at[4], corners[1]),
        (h_edge.at[0], h_sides.at[3], corners[2]),
        (h_edge.at[1], h_sides.at[2], corners[3]),
    ]
    h_copies = [
        start(src, dst, h_send.at[n], h_recv.at[n], peer) for n, (src, dst, peer) in enumerate(plan)
    ]
    has_up = jnp.where(s > 0, 1.0, 0.0)
    has_down = jnp.where(s < n_slab - 1, 1.0, 0.0)
    has_left = jnp.where(t > 0, 1.0, 0.0)
    has_right = jnp.where(t < n_tile - 1, 1.0, 0.0)
    ext[PITCH + 1 : PITCH + 33, :] = own[0:32, :]
    ext[2 * PITCH + 1 : 2 * PITCH + 33, :] = own[32:64, :]
    for copy in h_copies:
        copy.wait_recv()
    ext[1:33, :] = h_rows[0].astype(F32) * has_up
    ext[3 * PITCH + 1 : 3 * PITCH + 33, :] = h_rows[1].astype(F32) * has_down
    sides = [
        (0, has_left, ((PITCH, 0), (2 * PITCH, 1))),
        (1, has_right, ((PITCH + 33, 0), (2 * PITCH + 33, 1))),
        (2, has_up * has_left, ((0, 1),)),
        (3, has_up * has_right, ((33, 1),)),
        (4, has_down * has_left, ((3 * PITCH, 0),)),
        (5, has_down * has_right, ((3 * PITCH + 33, 0),)),
    ]
    for n, there, moves in sides:
        block = h_sides[n].astype(F32) * there
        for at, r in moves:
            ext[at : at + 1, :] = block[r : r + 1, :]

    tiles = ext[...].astype(BF16)
    lane = iota((256, 128), 1)
    source = (lane % 4) * 64 + (lane % 32) // 4
    for y in range(8):
        turn = as_bf16((iota((256, 128), 0) == source + 8 * y) & (lane < 96))
        rows = mm(tiles, turn)
        for tr in range(4):
            r = 8 * tr + y - 4
            if 0 <= r < 24:
                x0[PAD + PITCH * r : PAD + PITCH * r + PITCH, :] = rows[
                    PITCH * tr : PITCH * tr + PITCH, :
                ]
    n = 24 * PITCH
    lane = iota((n, 128), 1)
    x1[...] = jnp.where(
        lane < 32, x0[PAD : PAD + n, :], jnp.where(lane < 64, x0[PAD - 1 : PAD - 1 + n, :], x0[PAD + 1 : PAD + 1 + n, :])
    )

    group = iota((PITCH, 256), 0)
    inside = jnp.where(
        group == 0, has_left, jnp.where(group >= 33, has_right, 1.0)
    )[None]

    def finish(ref, value, outer):
        rows = value.shape[0] // PITCH
        kept = jnp.maximum(value, 0.0).reshape(rows, PITCH, 256) * inside
        ref[PAD : PAD + rows * PITCH, :] = (
            kept.reshape(rows * PITCH, 256).astype(BF16).astype(F32)
        )

        @pl.when(s == 0)
        def _():
            ref[PAD : PAD + outer * PITCH, :] = jnp.zeros((outer * PITCH, 256), F32)

        @pl.when(s == n_slab - 1)
        def _():
            ref[PAD + (rows - outer) * PITCH : PAD + rows * PITCH, :] = jnp.zeros(
                (outer * PITCH, 256), F32
            )

    m = 22 * PITCH
    wide = jnp.concatenate(
        [x1[PITCH * dy : PITCH * dy + m, :].astype(BF16) for dy in range(3)], axis=1
    )
    finish(e1, mm(wide, w1[...]), 3)

    def convolve(ref, layer, rows_in):
        n = rows_in * PITCH
        m = (rows_in - 2) * PITCH
        lane = iota((n, 128), 1)
        edge[0:n, :] = jnp.where(
            lane < 32,
            ref[PAD + 1 : PAD + 1 + n, 0:128],
            jnp.where(lane >= 96, ref[PAD - 1 : PAD - 1 + n, 128:256], 0.0),
        )
        wide = jnp.concatenate(
            [ref[PAD + PITCH * dy : PAD + PITCH * dy + m, :].astype(BF16) for dy in range(3)]
            + [edge[PITCH * dy : PITCH * dy + m, :].astype(BF16) for dy in range(3)],
            axis=1,
        )
        return mm(wide, wb[layer])

    finish(e2, convolve(e1, 0, 22), 2)
    finish(d1, convolve(e2, 1, 20), 1)
    m = 16 * PITCH
    d2 = jnp.maximum(convolve(d1, 2, 18) + e1[PAD + 3 * PITCH : PAD + 3 * PITCH + m, :], 0.0)
    last = jnp.concatenate(
        [d2.astype(BF16), x0[PAD + 4 * PITCH : PAD + 4 * PITCH + m, :].astype(BF16)], axis=1
    )
    own_group = (iota((PITCH, 256), 0) - 1 == iota((PITCH, 256), 1) // 8)[None]
    first_of = iota((16, m), 0) * PITCH
    of_row = as_bf16((iota((16, m), 1) >= first_of) & (iota((16, m), 1) < first_of + PITCH))
    for c in range(3):
        color_c = mm(last, wo[:, 256 * c : 256 * c + 256]).reshape(16, PITCH, 256)
        color_c = jnp.where(own_group, color_c, 0.0).reshape(m, 256).astype(BF16)
        out[c] = mm(of_row, color_c).astype(BF16)

    for copy in am_copies + a_copies + bm_copies + b_copies + h_copies:
        copy.wait_send()


def shards(
    density,
    brick_color,
    brick_row,
    brick_col,
    brick_steps,
    depth_flip,
    w_in,
    w_enc,
    w_dec,
    w_dec2,
    w_out,
):
    n_tile = lax.axis_size("tile")
    n_slab = lax.axis_size("slab")
    bricks = density.shape[0]
    slots = CAP * n_tile
    owned = 64 * n_slab
    taps = [jnp.transpose(w, (2, 3, 0, 1)).reshape(288, 32) for w in (w_enc, w_dec, w_dec2)]
    vmem = pl.BlockSpec(memory_space=pltpu.VMEM)
    dma = pltpu.SemaphoreType.DMA
    return pl.pallas_call(
        functools.partial(kernel, n_slab, n_tile),
        out_shape=jax.ShapeDtypeStruct((3, 16, 256), BF16),
        in_specs=[vmem] * 11,
        out_specs=vmem,
        scratch_shapes=[
            pltpu.VMEM((bricks, 256), BF16),
            pltpu.VMEM((slots, bricks), BF16),
            pltpu.VMEM((owned, slots), BF16),
            pltpu.VMEM((slots, 128), jnp.int16),
            pltpu.VMEM((slots, 128), jnp.int16),
            pltpu.VMEM((slots // 128, 16, 128), BF16),
            pltpu.VMEM((n_tile, 16, 128), BF16),
            pltpu.VMEM((owned, 256), F32),
            pltpu.VMEM((n_slab, 64, 128), jnp.int16),
            pltpu.VMEM((n_slab, 64, 128), jnp.int16),
            pltpu.VMEM((n_slab // 2, 16, 128), BF16),
            pltpu.VMEM((n_slab, 16, 128), BF16),
            pltpu.VMEM((n_slab, 64, 256), F32),
            pltpu.VMEM((64, 256), BF16),
            pltpu.VMEM((2, 16, 256), BF16),
            pltpu.VMEM((2, 32, 256), BF16),
            pltpu.VMEM((6, 16, 256), BF16),
            pltpu.VMEM((4 * PITCH, 256), F32),
            pltpu.VMEM((24 * PITCH + 2 * PAD, 128), F32),
            pltpu.VMEM((24 * PITCH, 128), F32),
            pltpu.VMEM((22 * PITCH + 2 * PAD, 256), F32),
            pltpu.VMEM((20 * PITCH + 2 * PAD, 256), F32),
            pltpu.VMEM((18 * PITCH + 2 * PAD, 256), F32),
            pltpu.VMEM((22 * PITCH, 128), F32),
            pltpu.VMEM((384, 256), BF16),
            pltpu.VMEM((3, 1152, 256), BF16),
            pltpu.VMEM((384, 768), BF16),
            dma((n_tile,)),
            dma((n_tile,)),
            dma((n_tile,)),
            dma((n_tile,)),
            dma((n_slab,)),
            dma((n_slab,)),
            dma((n_slab,)),
            dma((n_slab,)),
            dma((8,)),
            dma((8,)),
        ],
        compiler_params=pltpu.CompilerParams(
            collective_id=0, has_side_effects=True, vmem_limit_bytes=48 * 1024 * 1024
        ),
    )(
        density,
        brick_color,
        brick_row.reshape(1, bricks),
        brick_col.reshape(1, bricks),
        brick_steps.reshape(1, bricks),
        depth_flip,
        jnp.transpose(w_in, (2, 3, 1, 0)).reshape(9, 4, 32),
        *taps,
        w_out,
    )


def solution(mesh):
    return jax.shard_map(
        shards,
        mesh=mesh,
        in_specs=(
            P(("slab", "tile"), None),
            P(None, ("slab", "tile")),
            P(("slab", "tile")),
            P(("slab", "tile")),
            P(("slab", "tile")),
            P(None, "tile"),
            P(),
            P(),
            P(),
            P(),
            P(),
        ),
        out_specs=P(None, "slab", "tile"),
        check_vma=False,
    )
```

time: 193 us -> 57.3 us (0.30); the launches traced: 190 us -> 56.9 us
  starting transfers between devices: 71.6 us -> 0 us
  waiting for transfers between devices: 59.5 us -> 0 us
  Pallas kernels: 0 us -> 49.1 us
  local copies, waits for them, and re-layouts: 37 us -> 7.78 us
  other arithmetic: 11.7 us -> 0 us
  matrix products: 8.29 us -> 0 us
    pallas_call x0 -> x1, Pallas kernels: none -> 49.1 us  [shards(): pl.pallas_call(functools.partial(kernel, n_slab, n_tile), out_shape=jax.S...]
    ppermute x16 -> x0, starting transfers between devices: 39.4 us -> none  [the longest x8 25.6 us: with_halo(): lax.ppermute(lax.slice_in_dim(block, block.shape[dim] - width, None, axis...]
    all_to_all x3 -> x0, starting transfers between devices: 32.1 us -> none  [the longest x1 14.8 us: shards(): lax.all_to_all(canvas.reshape(1, owned, 256), 'slab', split_axis=1, conca...]
    all_to_all x3 -> x0, waiting for transfers between devices: 31.4 us -> none  [the longest x1 16.5 us: shards(): lax.all_to_all(canvas.reshape(1, owned, 256), 'slab', split_axis=1, conca...]
    ppermute x16 -> x0, waiting for transfers between devices: 28.1 us -> none  [the longest x8 26.6 us: with_halo(): lax.ppermute(lax.slice_in_dim(block, 0, width, axis=dim), axis, backward)]
    scatter x3 -> x0, local copies, waits for them, and re-layouts: 10.8 us -> none  [the longest x1 5.25 us: shards(): canvas = jnp.zeros((owned, 256), jnp.bfloat16).at[arrived_ids.reshape(-1)...]
    conv_general_dilated x4 -> x0, matrix products: 8.14 us -> none  [convolve(): lax.conv_general_dilated(field[None], kernel, (1, 1), 'VALID', dimension_...]
    conv_general_dilated x12 -> x0, local copies, waits for them, and re-layouts: 7.9 us -> none  [convolve(): lax.conv_general_dilated(field[None], kernel, (1, 1), 'VALID', dimension_...]
  transfers between devices with their start and end apart: 19 -> 0, of which waited for: 13 -> 0; matrix products, arithmetic and copies ran while one was open for 5% -> 0% of each run, Pallas kernels for 0% -> 0%
where the time goes in v1:
time: 57.3 us; the launch traced here: 56.9 us
  Pallas kernels  49.1 us (86%)
  local copies, waits for them, and re-layouts  7.78 us (14%)
    pallas_call x1, Pallas kernels, shards(): pl.pallas_call(functools.partial(kernel, n_slab, n_tile), out_shape=jax.S...  49.1 us
    unnamed x23, local copies, waits for them, and re-layouts  7.78 us

profile of v1, /device:TPU:1, one launch (start us, length us, event | category | flops | bytes accessed | tf_op | source)
XLA Modules:
  0.0 56.9 jit_solution(9725091827380829871)
XLA Ops:
  0.0 0.0 copy-start.5
  0.0 0.0 copy-start.8
  0.0 0.0 copy-start.7
  0.0 0.7 %copy-done.5 = bf16[32,4,3,3]{0,1,3,2:T(4,128)(2,1)S(1)} copy-done((bf16[32,4,3,3]{0,1,3,2:T(4,128)(2,1)S(1)}, bf16[32,4,3,3]{0,1,3,2:T(4,128)(2,1)}, u32[]{:S(2)}) %copy-start.5) | copy-done | bytes 2328
  0.7 0.0 copy-done.8
  0.7 0.0 copy-done.7
  0.7 0.0 copy-start
  0.7 1.0 %copy-done = bf16[512,512]{1,0:T(8,128)(2,1)S(1)} copy-done((bf16[512,512]{1,0:T(8,128)(2,1)S(1)}, bf16[512,512]{1,0:T(8,128)(2,1)}, u32[]{:S(2)}) %copy-start) | copy-done | bytes 524312
  1.8 0.0 copy-start.1
  1.8 0.9 %copy-done.1 = bf16[32,32,3,3]{1,0,3,2:T(8,128)(2,1)S(1)} copy-done((bf16[32,32,3,3]{1,0,3,2:T(8,128)(2,1)S(1)}, bf16[32,32,3,3]{1,0,3,2:T(8,128)(2,1)}, u32[]{:S(2)}) %copy-start.1) | copy-done | bytes 18456
  2.6 0.0 copy-start.2
  2.6 0.9 %copy-done.2 = bf16[32,32,3,3]{1,0,3,2:T(8,128)(2,1)S(1)} copy-done((bf16[32,32,3,3]{1,0,3,2:T(8,128)(2,1)S(1)}, bf16[32,32,3,3]{1,0,3,2:T(8,128)(2,1)}, u32[]{:S(2)}) %copy-start.2) | copy-done | bytes 18456
  3.5 0.0 copy-start.3
  3.5 0.9 %copy-done.3 = bf16[32,32,3,3]{1,0,3,2:T(8,128)(2,1)S(1)} copy-done((bf16[32,32,3,3]{1,0,3,2:T(8,128)(2,1)S(1)}, bf16[32,32,3,3]{1,0,3,2:T(8,128)(2,1)}, u32[]{:S(2)}) %copy-start.3) | copy-done | bytes 18456
  4.4 0.0 copy-start.4
  4.4 0.7 %copy-done.4 = s32[32,32]{1,0:T(8,128)S(1)} copy-done((s32[32,32]{1,0:T(8,128)S(1)}, s32[32,32]{1,0:T(8,128)}, u32[]{:S(2)}) %copy-start.4) | copy-done | bytes 4120
  5.1 0.0 copy-start.6
  5.1 0.7 %copy-done.6 = f32[3,512]{1,0:T(4,128)S(1)} copy-done((f32[3,512]{1,0:T(4,128)S(1)}, f32[3,512]{1,0:T(4,128)}, u32[]{:S(2)}) %copy-start.6) | copy-done | bytes 6168
  5.8 0.0 copy-start.9
  5.8 0.7 %copy-done.9 = s32[512]{0:T(512)S(1)} copy-done((s32[512]{0:T(512)S(1)}, s32[512]{0:T(512)}, u32[]{:S(2)}) %copy-start.9) | copy-done | bytes 2072
  6.5 0.0 copy-start.10
  6.5 0.7 %copy-done.10 = bf16[3,32]{1,0:T(4,128)(2,1)S(1)} copy-done((bf16[3,32]{1,0:T(4,128)(2,1)S(1)}, bf16[3,32]{1,0:T(4,128)(2,1)}, u32[]{:S(2)}) %copy-start.10) | copy-done | bytes 216
  7.2 49.1 %shard_map.109 = bf16[3,16,256]{2,1,0:T(8,128)(2,1)S(1)} custom-call(bf16[512,512]{1,0:T(8,128)(2,1)S(1)} %copy-done, f32[3,512]{1,0:T(4,128)S(1)} %copy-done.6, s32[1,512]{1,0:T(1,128)S(1)} %bitcast.19, s32[1,512]{1,0:T(1,128)S(1)} %bitcast.20, s32[1,512]{1,0:T(1,128)S(1)} %bitcast.21, s32[32,32]{1,0:T(8,128)S(1)} %copy-done.4, ...), custom_call_target="tpu_custom_call" | custom-call | tf_op jit(solution)/shard_map/pallas_call | solution.py:509
  56.3 0.6 %copy.13 = bf16[3,16,256]{2,1,0:T(8,128)(2,1)} copy(bf16[3,16,256]{2,1,0:T(8,128)(2,1)S(1)} %shard_map.109) | data formatting | bytes 49152
Async XLA Ops:
  0.0 0.7 %copy-start.5 = (bf16[32,4,3,3]{0,1,3,2:T(4,128)(2,1)S(1)}, bf16[32,4,3,3]{0,1,3,2:T(4,128)(2,1)}, u32[]{:S(2)}) copy-start(bf16[32,4,3,3]{0,1,3,2:T(4,128)(2,1)} %param.17) | copy-start | bytes 6916
  0.0 0.7 %copy-start.8 = (s32[512]{0:T(512)S(1)}, s32[512]{0:T(512)}, u32[]{:S(2)}) copy-start(s32[512]{0:T(512)} %param.14) | copy-start | bytes 6148
  0.0 0.7 %copy-start.7 = (s32[512]{0:T(512)S(1)}, s32[512]{0:T(512)}, u32[]{:S(2)}) copy-start(s32[512]{0:T(512)} %param.13) | copy-start | bytes 6148
  0.7 1.0 %copy-start = (bf16[512,512]{1,0:T(8,128)(2,1)S(1)}, bf16[512,512]{1,0:T(8,128)(2,1)}, u32[]{:S(2)}) copy-start(bf16[512,512]{1,0:T(8,128)(2,1)} %density.1) | copy-start | bytes 1572868
  1.8 0.9 %copy-start.1 = (bf16[32,32,3,3]{1,0,3,2:T(8,128)(2,1)S(1)}, bf16[32,32,3,3]{1,0,3,2:T(8,128)(2,1)}, u32[]{:S(2)}) copy-start(bf16[32,32,3,3]{1,0,3,2:T(8,128)(2,1)} %param.18) | copy-start | bytes 55300
  2.6 0.9 %copy-start.2 = (bf16[32,32,3,3]{1,0,3,2:T(8,128)(2,1)S(1)}, bf16[32,32,3,3]{1,0,3,2:T(8,128)(2,1)}, u32[]{:S(2)}) copy-start(bf16[32,32,3,3]{1,0,3,2:T(8,128)(2,1)} %param.19) | copy-start | bytes 55300
  3.5 0.9 %copy-start.3 = (bf16[32,32,3,3]{1,0,3,2:T(8,128)(2,1)S(1)}, bf16[32,32,3,3]{1,0,3,2:T(8,128)(2,1)}, u32[]{:S(2)}) copy-start(bf16[32,32,3,3]{1,0,3,2:T(8,128)(2,1)} %param.20) | copy-start | bytes 55300
  4.4 0.7 %copy-start.4 = (s32[32,32]{1,0:T(8,128)S(1)}, s32[32,32]{1,0:T(8,128)}, u32[]{:S(2)}) copy-start(s32[32,32]{1,0:T(8,128)} %flip.1) | copy-start | bytes 12292
  5.1 0.7 %copy-start.6 = (f32[3,512]{1,0:T(4,128)S(1)}, f32[3,512]{1,0:T(4,128)}, u32[]{:S(2)}) copy-start(f32[3,512]{1,0:T(4,128)} %color.1) | copy-start | bytes 18436
  5.8 0.7 %copy-start.9 = (s32[512]{0:T(512)S(1)}, s32[512]{0:T(512)}, u32[]{:S(2)}) copy-start(s32[512]{0:T(512)} %param.15) | copy-start | bytes 6148
  6.5 0.7 %copy-start.10 = (bf16[3,32]{1,0:T(4,128)(2,1)S(1)}, bf16[3,32]{1,0:T(4,128)(2,1)}, u32[]{:S(2)}) copy-start(bf16[3,32]{1,0:T(4,128)(2,1)} %w_out.1) | copy-start | bytes 580

commit v2 on v1

--- a/solution.py
+++ b/solution.py
@@ -86,13 +86,13 @@
             total = jnp.where(lane_x == x_in - kx + 1, tap, total)
         w1[128 * ky : 128 * ky + 128, :] = total.astype(BF16)
     spread_t = as_bf16(iota((256, 32), 1) == iota((256, 32), 0) % 32)
-    same_x = iota((256, 256), 0) // 32 == iota((256, 256), 1) % 8
-    row = iota((128, 256), 0)
+    same_x = iota((256, 128), 0) // 32 == iota((256, 128), 1) % 8
+    row = iota((128, 128), 0)
     for c in range(3):
-        along = mm_nt(spread_t, jnp.broadcast_to(w_out[c : c + 1, :], (256, 32)))
-        wo[0:256, 256 * c : 256 * c + 256] = jnp.where(same_x, along, 0.0).astype(BF16)
-        own = (row < 32) & (row % 4 == c) & (row // 4 == iota((128, 256), 1) % 8)
-        wo[256:384, 256 * c : 256 * c + 256] = as_bf16(own)
+        along = mm_nt(spread_t, jnp.broadcast_to(w_out[c : c + 1, :], (128, 32)))
+        wo[0:256, 128 * c : 128 * c + 128] = jnp.where(same_x, along, 0.0).astype(BF16)
+        own = (row < 32) & (row % 4 == c) & (row // 4 == iota((128, 128), 1) % 8)
+        wo[256:384, 128 * c : 128 * c + 128] = as_bf16(own)
 
 
 def ray_march(density, steps, part):
@@ -125,6 +125,23 @@
 def kernel(
     n_slab,
     n_tile,
+    *refs,
+):
+    inputs, staged = refs[:11], refs[12:23]
+    out, load, refs = refs[11], refs[23], refs[24:]
+    loads = [
+        pltpu.make_async_copy(src, dst, load.at[n])
+        for n, (src, dst) in enumerate(zip(inputs, staged))
+    ]
+    for n in (3, 2, 1, 0, 4, 5, 6, 7, 8, 9, 10):
+        loads[n].start()
+    run(n_slab, n_tile, loads, *staged, out, *refs)
+
+
+def run(
+    n_slab,
+    n_tile,
+    loads,
     density,
     color,
     brick_row,
@@ -143,6 +160,7 @@
     a_out,
     a_in,
     am_out,
+    am_land,
     am_in,
     canvas,
     b_out,
@@ -164,6 +182,7 @@
     w1,
     wb,
     wo,
+    fo,
     am_send,
     am_recv,
     a_send,
@@ -200,6 +219,8 @@
     for peer in greeted:
         pl.semaphore_signal(barrier, inc=1, device_id=peer, device_id_type=MESH)
 
+    for n in (1, 2, 3):
+        loads[n].wait()
     col = brick_col[...]
     row = brick_row[...]
     rel = (col // 32 - t + n_tile) % n_tile
@@ -210,23 +231,18 @@
     slot = rel * CAP + rank
     place[...] = as_bf16(iota((slots, bricks), 0) == slot)
     block = (row // 2 - s + n_slab) % n_slab
-    tile_hi = (block * 2 + row % 2 + 1).astype(F32)
-    tile_lo = (col % 32).astype(F32)
+    tile_id = (block * 64 + row % 2 * 32 + col % 32 + 1).astype(F32)
+    in_slot = iota((CAP, bricks), 0) == rank
     tints = color[...]
-    tints_hi = tints.astype(BF16).astype(F32)
-    tints_lo = tints - tints_hi
-    field = iota((16, bricks), 0)
-    meta = jnp.zeros((16, bricks), F32)
-    for c in range(3):
-        meta = jnp.where(field == 2 * c, tints_hi[c : c + 1, :], meta)
-        meta = jnp.where(field == 2 * c + 1, tints_lo[c : c + 1, :], meta)
-    meta = jnp.where(field == 6, tile_hi, meta)
-    meta = jnp.where(field == 7, tile_lo, meta)
-    meta = jnp.where(field == 8, 1.0, meta)
-    sent_meta = mm_nt(meta.astype(BF16), place[...]).astype(BF16)
-    for g in range(slots // 128):
-        am_out[g] = sent_meta[:, 128 * g : 128 * g + 128]
-    am_in[0] = am_out[0]
+    fields = [tints[0:1, :], tints[1:2, :], tints[2:3, :], tile_id]
+    spread = jnp.concatenate([jnp.where(in_slot, f, 0.0) for f in fields], axis=0)
+    high = spread.astype(BF16)
+    low = (spread - high.astype(F32)).astype(BF16)
+    owner = as_bf16(mine)
+    notes = mm_nt(owner, high) + mm_nt(owner, low)
+    for i in range(1, n_tile):
+        am_out[i] = notes[i : i + 1, :]
+    am_in[0:1, :] = notes[0:1, :]
 
     pl.semaphore_wait(barrier, len(greeted))
 
@@ -243,10 +259,12 @@
         return copy
 
     am_copies = [
-        start(am_out.at[i // 4], am_in.at[i], am_send.at[i], am_recv.at[i], tile_peer(i))
+        start(am_out.at[i], am_land.at[i], am_send.at[i], am_recv.at[i], tile_peer(i))
         for i in range(1, n_tile)
     ]
 
+    loads[0].wait()
+    loads[4].wait()
     ray_march(density, steps, part)
     a_copies = []
     for g in range(slots // 128):
@@ -266,15 +284,24 @@
 
     for copy in am_copies:
         copy.wait_recv()
-    lane = iota((16, 128), 1)
-    groups = []
-    for g in range(slots // 128):
-        got = am_in[4 * g].astype(F32)
-        for q in range(1, 4):
-            got = jnp.where(lane // 32 == q, am_in[4 * g + q].astype(F32), got)
-        groups.append(got)
-    arrived = jnp.concatenate(groups, axis=1)
-    tile_id = (32.0 * arrived[6:7, :] + arrived[7:8, :] - 32.0).astype(jnp.int32)
+    for i in range(1, n_tile):
+        am_in[i : i + 1, :] = am_land[i]
+    notes = am_in[...]
+    high = notes.astype(BF16)
+    both = jnp.concatenate([high, (notes - high.astype(F32)).astype(BF16)], axis=0)
+    from_peer = iota((2 * n_tile, slots), 0) % n_tile == iota((2 * n_tile, slots), 1) // CAP
+    in_row = iota((128, slots), 0) - iota((128, slots), 1) % CAP
+    field = iota((16, slots), 0)
+    arrived = jnp.zeros((16, slots), F32)
+    for f in range(4):
+        here = jnp.where(from_peer, mm(both, as_bf16(in_row == CAP * f)), 0.0)
+        high = jnp.sum(here[0:n_tile], axis=0, keepdims=True)
+        low = jnp.sum(here[n_tile:], axis=0, keepdims=True)
+        if f < 3:
+            arrived = jnp.where(field == 2 * f, high, jnp.where(field == 2 * f + 1, low, arrived))
+        else:
+            tile_id = (high + low).astype(jnp.int32) - 1
+            arrived = jnp.where((field == 8) & (tile_id >= 0), 1.0, arrived)
     canvas_of[...] = as_bf16(iota((owned, slots), 0) == tile_id)
     tile_meta = mm_nt(arrived.astype(BF16), canvas_of[...]).astype(BF16)
     for g in range(n_slab // 2):
@@ -285,6 +312,8 @@
         for j in range(1, n_slab)
     ]
 
+    for n in (6, 7, 8, 9, 10):
+        loads[n].wait()
     build_weights(w_in, (w_enc, w_dec, w_dec2), w_out, w1, wb, wo)
     ext[...] = jnp.zeros(ext.shape, F32)
     for ref in (x0, e1, e2, d1):
@@ -322,6 +351,7 @@
         both = mm_tn(bm_in[j], choose)
         tint[j] = both[64 * (j % 2) : 64 * (j % 2) + 64, :]
 
+    loads[5].wait()
     flips = flip[pl.ds(2 * s, 2), :]
     same = iota((32, 32), 0) == iota((32, 32), 1)
     flipped = (
@@ -473,13 +503,16 @@
     last = jnp.concatenate(
         [d2.astype(BF16), x0[PAD + 4 * PITCH : PAD + 4 * PITCH + m, :].astype(BF16)], axis=1
     )
-    own_group = (iota((PITCH, 256), 0) - 1 == iota((PITCH, 256), 1) // 8)[None]
-    first_of = iota((16, m), 0) * PITCH
-    of_row = as_bf16((iota((16, m), 1) >= first_of) & (iota((16, m), 1) < first_of + PITCH))
     for c in range(3):
-        color_c = mm(last, wo[:, 256 * c : 256 * c + 256]).reshape(16, PITCH, 256)
-        color_c = jnp.where(own_group, color_c, 0.0).reshape(m, 256).astype(BF16)
-        out[c] = mm(of_row, color_c).astype(BF16)
+        fo[c] = mm(last, wo[:, 128 * c : 128 * c + 128])
+    of_group = iota((16, 128), 1) // 8
+    for c in range(3):
+        for half in range(2):
+            found = jnp.zeros((16, 128), F32)
+            for g in range(16):
+                rows = pl.ds(1 + 16 * half + g, 16, stride=PITCH)
+                found = jnp.where(of_group == g, fo[c, rows, :], found)
+            out[c, :, 128 * half : 128 * half + 128] = found.astype(BF16)
 
     for copy in am_copies + a_copies + bm_copies + b_copies + h_copies:
         copy.wait_send()
@@ -506,19 +539,33 @@
     taps = [jnp.transpose(w, (2, 3, 0, 1)).reshape(288, 32) for w in (w_enc, w_dec, w_dec2)]
     vmem = pl.BlockSpec(memory_space=pltpu.VMEM)
     dma = pltpu.SemaphoreType.DMA
+    operands = (
+        density,
+        brick_color,
+        brick_row.reshape(1, bricks),
+        brick_col.reshape(1, bricks),
+        brick_steps.reshape(1, bricks),
+        depth_flip,
+        jnp.transpose(w_in, (2, 3, 1, 0)).reshape(9, 4, 32),
+        *taps,
+        w_out,
+    )
     return pl.pallas_call(
         functools.partial(kernel, n_slab, n_tile),
         out_shape=jax.ShapeDtypeStruct((3, 16, 256), BF16),
-        in_specs=[vmem] * 11,
+        in_specs=[pl.BlockSpec(memory_space=pltpu.HBM)] * 11,
         out_specs=vmem,
-        scratch_shapes=[
+        scratch_shapes=[pltpu.VMEM(x.shape, x.dtype) for x in operands]
+        + [
+            dma((11,)),
             pltpu.VMEM((bricks, 256), BF16),
             pltpu.VMEM((slots, bricks), BF16),
             pltpu.VMEM((owned, slots), BF16),
             pltpu.VMEM((slots, 128), jnp.int16),
             pltpu.VMEM((slots, 128), jnp.int16),
-            pltpu.VMEM((slots // 128, 16, 128), BF16),
-            pltpu.VMEM((n_tile, 16, 128), BF16),
+            pltpu.VMEM((n_tile, 1, 128), F32),
+            pltpu.VMEM((n_tile, 1, 128), F32),
+            pltpu.VMEM((n_tile, 128), F32),
             pltpu.VMEM((owned, 256), F32),
             pltpu.VMEM((n_slab, 64, 128), jnp.int16),
             pltpu.VMEM((n_slab, 64, 128), jnp.int16),
@@ -538,7 +585,8 @@
             pltpu.VMEM((22 * PITCH, 128), F32),
             pltpu.VMEM((384, 256), BF16),
             pltpu.VMEM((3, 1152, 256), BF16),
-            pltpu.VMEM((384, 768), BF16),
+            pltpu.VMEM((384, 384), BF16),
+            pltpu.VMEM((3, 16 * PITCH, 128), F32),
             dma((n_tile,)),
             dma((n_tile,)),
             dma((n_tile,)),
@@ -551,19 +599,9 @@
             dma((8,)),
         ],
         compiler_params=pltpu.CompilerParams(
-            collective_id=0, has_side_effects=True, vmem_limit_bytes=48 * 1024 * 1024
+            collective_id=0, has_side_effects=True, vmem_limit_bytes=62 * 1024 * 1024
         ),
-    )(
-        density,
-        brick_color,
-        brick_row.reshape(1, bricks),
-        brick_col.reshape(1, bricks),
-        brick_steps.reshape(1, bricks),
-        depth_flip,
-        jnp.transpose(w_in, (2, 3, 1, 0)).reshape(9, 4, 32),
-        *taps,
-        w_out,
-    )
+    )(*operands)
 
 
 def solution(mesh):

time: 57.3 us -> 49.4 us (0.86)
  local copies, waits for them, and re-layouts: 7.78 us -> 1.35 us
  Pallas kernels: 49.1 us -> 47.9 us
    unnamed x23 -> x1, local copies, waits for them, and re-layouts: 7.78 us -> 1.35 us
    pallas_call x1, Pallas kernels: 49.1 us -> 47.9 us  [shards(): pl.pallas_call(functools.partial(kernel, n_slab, n_tile), out_shape=jax.S...]
where the time goes in v2:
time: 49.4 us; the launch traced here: 49.2 us
  Pallas kernels  47.9 us (97%)
  local copies, waits for them, and re-layouts  1.35 us (3%)
    pallas_call x1, Pallas kernels, shards(): pl.pallas_call(functools.partial(kernel, n_slab, n_tile), out_shape=jax.S...  47.9 us
    unnamed x1, local copies, waits for them, and re-layouts  1.35 us

profile of v2, /device:TPU:1, one launch (start us, length us, event | category | flops | bytes accessed | tf_op | source)
XLA Modules:
  0.0 49.2 jit_solution(2254509459569576283)
XLA Ops:
  0.0 47.9 %shard_map.109 = bf16[3,16,256]{2,1,0:T(8,128)(2,1)} custom-call(bf16[512,512]{1,0:T(8,128)(2,1)} %refs_0_.1, f32[3,512]{1,0:T(4,128)} %refs_1_.1, s32[1,512]{1,0:T(1,128)} %bitcast.19, s32[1,512]{1,0:T(1,128)} %bitcast.20, s32[1,512]{1,0:T(1,128)} %bitcast.21, s32[32,32]{1,0:T(8,128)} %refs_5_.1, bf16[9,4,32]{2,1,0:T(4,128)(2,1)} %bitcast.18, ...), custom_call_target="tpu_custom_call" | custom-call | tf_op jit(solution)/shard_map/pallas_call | solution.py:553
  47.9 1.3 %copy.13 = bf16[3,16,256]{2,1,0:T(8,128)(2,1)} copy(bf16[3,16,256]{2,1,0:T(8,128)(2,1)} %shard_map.109) | data formatting | bytes 49152

commit v3 on v2

--- a/solution.py
+++ b/solution.py
@@ -122,6 +122,90 @@
         part[rows, :] = split((value + 0.5).astype(jnp.int32))
 
 
+def denoise(
+    top, bottom, has_left, has_right, ext, x0, x1, e1, e2, d1, edge, w1, wb, wo, fo, out
+):
+    tiles = ext[...].astype(BF16)
+    lane = iota((256, 128), 1)
+    source = (lane % 4) * 64 + (lane % 32) // 4
+    for y in range(8):
+        turn = as_bf16((iota((256, 128), 0) == source + 8 * y) & (lane < 96))
+        rows = mm(tiles, turn)
+        for tr in range(4):
+            r = 8 * tr + y - 4
+            if 0 <= r < 24:
+                x0[PAD + PITCH * r : PAD + PITCH * r + PITCH, :] = rows[
+                    PITCH * tr : PITCH * tr + PITCH, :
+                ]
+    n = 24 * PITCH
+    lane = iota((n, 128), 1)
+    x1[...] = jnp.where(
+        lane < 32, x0[PAD : PAD + n, :], jnp.where(lane < 64, x0[PAD - 1 : PAD - 1 + n, :], x0[PAD + 1 : PAD + 1 + n, :])
+    )
+
+    group = iota((PITCH, 256), 0)
+    inside = jnp.where(
+        group == 0, has_left, jnp.where(group >= 33, has_right, 1.0)
+    )[None]
+
+    def finish(ref, value, outer):
+        rows = value.shape[0] // PITCH
+        kept = jnp.maximum(value, 0.0).reshape(rows, PITCH, 256) * inside
+        ref[PAD : PAD + rows * PITCH, :] = (
+            kept.reshape(rows * PITCH, 256).astype(BF16).astype(F32)
+        )
+
+        @pl.when(top)
+        def _():
+            ref[PAD : PAD + outer * PITCH, :] = jnp.zeros((outer * PITCH, 256), F32)
+
+        @pl.when(bottom)
+        def _():
+            ref[PAD + (rows - outer) * PITCH : PAD + rows * PITCH, :] = jnp.zeros(
+                (outer * PITCH, 256), F32
+            )
+
+    m = 22 * PITCH
+    wide = jnp.concatenate(
+        [x1[PITCH * dy : PITCH * dy + m, :].astype(BF16) for dy in range(3)], axis=1
+    )
+    finish(e1, mm(wide, w1[...]), 3)
+
+    def convolve(ref, layer, rows_in):
+        n = rows_in * PITCH
+        m = (rows_in - 2) * PITCH
+        lane = iota((n, 128), 1)
+        edge[0:n, :] = jnp.where(
+            lane < 32,
+            ref[PAD + 1 : PAD + 1 + n, 0:128],
+            jnp.where(lane >= 96, ref[PAD - 1 : PAD - 1 + n, 128:256], 0.0),
+        )
+        wide = jnp.concatenate(
+            [ref[PAD + PITCH * dy : PAD + PITCH * dy + m, :].astype(BF16) for dy in range(3)]
+            + [edge[PITCH * dy : PITCH * dy + m, :].astype(BF16) for dy in range(3)],
+            axis=1,
+        )
+        return mm(wide, wb[layer])
+
+    finish(e2, convolve(e1, 0, 22), 2)
+    finish(d1, convolve(e2, 1, 20), 1)
+    m = 16 * PITCH
+    d2 = jnp.maximum(convolve(d1, 2, 18) + e1[PAD + 3 * PITCH : PAD + 3 * PITCH + m, :], 0.0)
+    last = jnp.concatenate(
+        [d2.astype(BF16), x0[PAD + 4 * PITCH : PAD + 4 * PITCH + m, :].astype(BF16)], axis=1
+    )
+    for c in range(3):
+        fo[c] = mm(last, wo[:, 128 * c : 128 * c + 128])
+    of_group = iota((16, 128), 1) // 8
+    for c in range(3):
+        for half in range(2):
+            found = jnp.zeros((16, 128), F32)
+            for g in range(16):
+                rows = pl.ds(1 + 16 * half + g, 16, stride=PITCH)
+                found = jnp.where(of_group == g, fo[c, rows, :], found)
+            out[c, :, 128 * half : 128 * half + 128] = found.astype(BF16)
+
+
 def kernel(
     n_slab,
     n_tile,
@@ -133,8 +217,6 @@
         pltpu.make_async_copy(src, dst, load.at[n])
         for n, (src, dst) in enumerate(zip(inputs, staged))
     ]
-    for n in (3, 2, 1, 0, 4, 5, 6, 7, 8, 9, 10):
-        loads[n].start()
     run(n_slab, n_tile, loads, *staged, out, *refs)
 
 
@@ -219,6 +301,8 @@
     for peer in greeted:
         pl.semaphore_signal(barrier, inc=1, device_id=peer, device_id_type=MESH)
 
+    for n in (3, 2, 1, 0, 4, 5, 6, 7, 8, 9, 10):
+        loads[n].start()
     for n in (1, 2, 3):
         loads[n].wait()
     col = brick_col[...]
@@ -244,8 +328,6 @@
         am_out[i] = notes[i : i + 1, :]
     am_in[0:1, :] = notes[0:1, :]
 
-    pl.semaphore_wait(barrier, len(greeted))
-
     def start(src, dst, send, recv, peer):
         copy = pltpu.make_async_remote_copy(
             src_ref=src,
@@ -258,33 +340,39 @@
         copy.start()
         return copy
 
-    am_copies = [
-        start(am_out.at[i], am_land.at[i], am_send.at[i], am_recv.at[i], tile_peer(i))
-        for i in range(1, n_tile)
-    ]
-
     loads[0].wait()
     loads[4].wait()
     ray_march(density, steps, part)
-    a_copies = []
     for g in range(slots // 128):
         a_out[128 * g : 128 * g + 128, :] = join(
             mm(place[128 * g : 128 * g + 128, :], part[...])
         )
-        for i in range(4 * g, 4 * g + 4):
-            span = pl.ds(CAP * i, CAP)
-            if i == 0:
-                a_in[0:CAP, :] = a_out[0:CAP, :]
-            else:
-                a_copies.append(
-                    start(
-                        a_out.at[span], a_in.at[span], a_send.at[i], a_recv.at[i], tile_peer(i)
-                    )
-                )
-
-    for copy in am_copies:
-        copy.wait_recv()
+    a_in[0:CAP, :] = a_out[0:CAP, :]
+
+    pl.semaphore_wait(barrier, len(greeted))
+    across = range(1, n_tile)
+    am_copies = {
+        i: start(am_out.at[i], am_land.at[i], am_send.at[i], am_recv.at[i], tile_peer(i))
+        for i in across
+    }
+    a_copies = {}
+    for i in across:
+        span = pl.ds(CAP * i, CAP)
+        a_copies[i] = start(
+            a_out.at[span], a_in.at[span], a_send.at[i], a_recv.at[i], tile_peer(i)
+        )
+
+    for n in (6, 7, 8, 9, 10):
+        loads[n].wait()
+    build_weights(w_in, (w_enc, w_dec, w_dec2), w_out, w1, wb, wo)
+    ext[...] = jnp.zeros(ext.shape, F32)
+    for ref in (x0, e1, e2, d1):
+        width = ref.shape[1]
+        ref[0:PAD, :] = jnp.zeros((PAD, width), F32)
+        ref[ref.shape[0] - PAD :, :] = jnp.zeros((PAD, width), F32)
+
     for i in range(1, n_tile):
+        am_copies[i].wait_recv()
         am_in[i : i + 1, :] = am_land[i]
     notes = am_in[...]
     high = notes.astype(BF16)
@@ -312,35 +400,34 @@
         for j in range(1, n_slab)
     ]
 
-    for n in (6, 7, 8, 9, 10):
-        loads[n].wait()
-    build_weights(w_in, (w_enc, w_dec, w_dec2), w_out, w1, wb, wo)
-    ext[...] = jnp.zeros(ext.shape, F32)
-    for ref in (x0, e1, e2, d1):
-        width = ref.shape[1]
-        ref[0:PAD, :] = jnp.zeros((PAD, width), F32)
-        ref[ref.shape[0] - PAD :, :] = jnp.zeros((PAD, width), F32)
-
     chunk = min(256, slots)
-    for k in range(slots // chunk):
-        for i in range(max(1, k * chunk // CAP), (k + 1) * chunk // CAP):
-            a_copies[i - 1].wait_recv()
-        span = slice(k * chunk, (k + 1) * chunk)
-        term = mm(canvas_of[:, span], split(a_in[span, :].astype(jnp.int32) + 32768))
-        if k == 0:
-            canvas[...] = term
-        else:
-            canvas[...] += term
+    spans = [slice(k * chunk, (k + 1) * chunk) for k in (0, 1, 3, 2) if k * chunk < slots]
+    for k, span in enumerate(spans):
+        for i in range(max(1, span.start // CAP), span.stop // CAP):
+            a_copies[i].wait_recv()
+        came = split(a_in[span, :].astype(jnp.int32) + 32768)
+        if k + 1 < len(spans):
+            term = mm(canvas_of[:, span], came)
+            if k == 0:
+                canvas[...] = term
+            else:
+                canvas[...] += term
     b_copies = []
-    for j in range(n_slab):
-        piece = join(canvas[64 * j : 64 * j + 64, :])
-        if j == 0:
-            b_in[0] = piece
-        else:
-            b_out[j] = piece
-            b_copies.append(
-                start(b_out.at[j], b_in.at[j], b_send.at[j], b_recv.at[j], slab_peer(j))
-            )
+    for pair in range(n_slab // 2):
+        rows = slice(128 * pair, 128 * pair + 128)
+        levels = mm(canvas_of[rows, span], came)
+        if len(spans) > 1:
+            levels = levels + canvas[rows, :]
+        levels = join(levels)
+        for j in (2 * pair, 2 * pair + 1):
+            piece = levels[64 * (j % 2) : 64 * (j % 2) + 64, :]
+            if j == 0:
+                b_in[0] = piece
+            else:
+                b_out[j] = piece
+                b_copies.append(
+                    start(b_out.at[j], b_in.at[j], b_send.at[j], b_recv.at[j], slab_peer(j))
+                )
 
     for copy in bm_copies:
         copy.wait_recv()
@@ -399,14 +486,14 @@
         ).astype(BF16)
     up, down, left, right = near(-1, 0), near(1, 0), near(0, -1), near(0, 1)
     plan = [
-        (h_own.at[pl.ds(0, 32)], h_rows.at[1], up),
-        (h_own.at[pl.ds(32, 32)], h_rows.at[0], down),
-        (h_edge.at[0], h_sides.at[1], left),
-        (h_edge.at[1], h_sides.at[0], right),
         (h_edge.at[0], h_sides.at[5], corners[0]),
         (h_edge.at[1], h_sides.at[4], corners[1]),
         (h_edge.at[0], h_sides.at[3], corners[2]),
         (h_edge.at[1], h_sides.at[2], corners[3]),
+        (h_edge.at[0], h_sides.at[1], left),
+        (h_edge.at[1], h_sides.at[0], right),
+        (h_own.at[pl.ds(0, 32)], h_rows.at[1], up),
+        (h_own.at[pl.ds(32, 32)], h_rows.at[0], down),
     ]
     h_copies = [
         start(src, dst, h_send.at[n], h_recv.at[n], peer) for n, (src, dst, peer) in enumerate(plan)
@@ -434,87 +521,11 @@
         for at, r in moves:
             ext[at : at + 1, :] = block[r : r + 1, :]
 
-    tiles = ext[...].astype(BF16)
-    lane = iota((256, 128), 1)
-    source = (lane % 4) * 64 + (lane % 32) // 4
-    for y in range(8):
-        turn = as_bf16((iota((256, 128), 0) == source + 8 * y) & (lane < 96))
-        rows = mm(tiles, turn)
-        for tr in range(4):
-            r = 8 * tr + y - 4
-            if 0 <= r < 24:
-                x0[PAD + PITCH * r : PAD + PITCH * r + PITCH, :] = rows[
-                    PITCH * tr : PITCH * tr + PITCH, :
-                ]
-    n = 24 * PITCH
-    lane = iota((n, 128), 1)
-    x1[...] = jnp.where(
-        lane < 32, x0[PAD : PAD + n, :], jnp.where(lane < 64, x0[PAD - 1 : PAD - 1 + n, :], x0[PAD + 1 : PAD + 1 + n, :])
-    )
-
-    group = iota((PITCH, 256), 0)
-    inside = jnp.where(
-        group == 0, has_left, jnp.where(group >= 33, has_right, 1.0)
-    )[None]
-
-    def finish(ref, value, outer):
-        rows = value.shape[0] // PITCH
-        kept = jnp.maximum(value, 0.0).reshape(rows, PITCH, 256) * inside
-        ref[PAD : PAD + rows * PITCH, :] = (
-            kept.reshape(rows * PITCH, 256).astype(BF16).astype(F32)
-        )
-
-        @pl.when(s == 0)
-        def _():
-            ref[PAD : PAD + outer * PITCH, :] = jnp.zeros((outer * PITCH, 256), F32)
-
-        @pl.when(s == n_slab - 1)
-        def _():
-            ref[PAD + (rows - outer) * PITCH : PAD + rows * PITCH, :] = jnp.zeros(
-                (outer * PITCH, 256), F32
-            )
-
-    m = 22 * PITCH
-    wide = jnp.concatenate(
-        [x1[PITCH * dy : PITCH * dy + m, :].astype(BF16) for dy in range(3)], axis=1
-    )
-    finish(e1, mm(wide, w1[...]), 3)
-
-    def convolve(ref, layer, rows_in):
-        n = rows_in * PITCH
-        m = (rows_in - 2) * PITCH
-        lane = iota((n, 128), 1)
-        edge[0:n, :] = jnp.where(
-            lane < 32,
-            ref[PAD + 1 : PAD + 1 + n, 0:128],
-            jnp.where(lane >= 96, ref[PAD - 1 : PAD - 1 + n, 128:256], 0.0),
-        )
-        wide = jnp.concatenate(
-            [ref[PAD + PITCH * dy : PAD + PITCH * dy + m, :].astype(BF16) for dy in range(3)]
-            + [edge[PITCH * dy : PITCH * dy + m, :].astype(BF16) for dy in range(3)],
-            axis=1,
-        )
-        return mm(wide, wb[layer])
-
-    finish(e2, convolve(e1, 0, 22), 2)
-    finish(d1, convolve(e2, 1, 20), 1)
-    m = 16 * PITCH
-    d2 = jnp.maximum(convolve(d1, 2, 18) + e1[PAD + 3 * PITCH : PAD + 3 * PITCH + m, :], 0.0)
-    last = jnp.concatenate(
-        [d2.astype(BF16), x0[PAD + 4 * PITCH : PAD + 4 * PITCH + m, :].astype(BF16)], axis=1
-    )
-    for c in range(3):
-        fo[c] = mm(last, wo[:, 128 * c : 128 * c + 128])
-    of_group = iota((16, 128), 1) // 8
-    for c in range(3):
-        for half in range(2):
-            found = jnp.zeros((16, 128), F32)
-            for g in range(16):
-                rows = pl.ds(1 + 16 * half + g, 16, stride=PITCH)
-                found = jnp.where(of_group == g, fo[c, rows, :], found)
-            out[c, :, 128 * half : 128 * half + 128] = found.astype(BF16)
-
-    for copy in am_copies + a_copies + bm_copies + b_copies + h_copies:
+    denoise(
+        s == 0, s == n_slab - 1, has_left, has_right, ext, x0, x1, e1, e2, d1, edge, w1, wb, wo, fo, out
+    )
+
+    for copy in [*am_copies.values(), *a_copies.values()] + bm_copies + b_copies + h_copies:
         copy.wait_send()
 
 

time: 49.4 us -> 48.6 us (0.984)
  Pallas kernels: 47.9 us -> 47.1 us
    pallas_call x1, Pallas kernels: 47.9 us -> 47.1 us  [shards(): pl.pallas_call(functools.partial(kernel, n_slab, n_tile), out_shape=jax.S...]
where the time goes in v3:
time: 48.6 us; the launch traced here: 48.4 us
  Pallas kernels  47.1 us (97%)
  local copies, waits for them, and re-layouts  1.35 us (3%)
    pallas_call x1, Pallas kernels, shards(): pl.pallas_call(functools.partial(kernel, n_slab, n_tile), out_shape=jax.S...  47.1 us
    unnamed x1, local copies, waits for them, and re-layouts  1.35 us

profile of v3, /device:TPU:1, one launch (start us, length us, event | category | flops | bytes accessed | tf_op | source)
XLA Modules:
  0.0 48.4 jit_solution(16050734200647516993)
XLA Ops:
  0.0 47.1 %shard_map.109 = bf16[3,16,256]{2,1,0:T(8,128)(2,1)} custom-call(bf16[512,512]{1,0:T(8,128)(2,1)} %refs_0_.1, f32[3,512]{1,0:T(4,128)} %refs_1_.1, s32[1,512]{1,0:T(1,128)} %bitcast.19, s32[1,512]{1,0:T(1,128)} %bitcast.20, s32[1,512]{1,0:T(1,128)} %bitcast.21, s32[32,32]{1,0:T(8,128)} %refs_5_.1, bf16[9,4,32]{2,1,0:T(4,128)(2,1)} %bitcast.18, ...), custom_call_target="tpu_custom_call" | custom-call | tf_op jit(solution)/shard_map/pallas_call | solution.py:564
  47.1 1.3 %copy.13 = bf16[3,16,256]{2,1,0:T(8,128)(2,1)} copy(bf16[3,16,256]{2,1,0:T(8,128)(2,1)} %shard_map.109) | data formatting | bytes 49152

commit v4 on v3

--- a/solution.py
+++ b/solution.py
@@ -70,10 +70,10 @@
                 for kx in range(3):
                     total = jnp.where(lane_x == x_in - kx + 1, taps[kx], total)
                 wb[layer, base + 32 * x_in : base + 32 * x_in + 32, :] = total.astype(BF16)
-            edge = 768 + 128 * ky
-            wb[layer, edge : edge + 32, :] = jnp.where(lane_x == 7, taps[2], 0.0).astype(BF16)
-            wb[layer, edge + 32 : edge + 96, :] = jnp.zeros((64, 256), BF16)
-            wb[layer, edge + 96 : edge + 128, :] = jnp.where(lane_x == 0, taps[0], 0.0).astype(BF16)
+            right, left = ((768, 864), (832, 800), (896, 992))[ky]
+            wb[layer, right : right + 32, :] = jnp.where(lane_x == 7, taps[2], 0.0).astype(BF16)
+            wb[layer, left : left + 32, :] = jnp.where(lane_x == 0, taps[0], 0.0).astype(BF16)
+        wb[layer, 928:992, :] = jnp.zeros((64, 256), BF16)
     row = iota((128, 256), 0)
     lane_x = iota((128, 256), 1) // 32
     third = row // 32
@@ -87,12 +87,9 @@
         w1[128 * ky : 128 * ky + 128, :] = total.astype(BF16)
     spread_t = as_bf16(iota((256, 32), 1) == iota((256, 32), 0) % 32)
     same_x = iota((256, 128), 0) // 32 == iota((256, 128), 1) % 8
-    row = iota((128, 128), 0)
     for c in range(3):
         along = mm_nt(spread_t, jnp.broadcast_to(w_out[c : c + 1, :], (128, 32)))
         wo[0:256, 128 * c : 128 * c + 128] = jnp.where(same_x, along, 0.0).astype(BF16)
-        own = (row < 32) & (row % 4 == c) & (row // 4 == iota((128, 128), 1) % 8)
-        wo[256:384, 128 * c : 128 * c + 128] = as_bf16(own)
 
 
 def ray_march(density, steps, part):
@@ -122,8 +119,25 @@
         part[rows, :] = split((value + 0.5).astype(jnp.int32))
 
 
+def lay_out(tiles, base):
+    row = iota((256, 384), 0)
+    lane = iota((256, 384), 1)
+    source = lane // 128 * 64 + lane % 8
+    of_tile = iota((16, 128), 0) == iota((16, 128), 1) // 8
+    for y in range(8):
+        spread = mm(tiles, as_bf16(row == source + 8 * y))
+        for tr in range(2):
+            for half in range(2):
+                first = 32 * tr + 16 * half
+                for c in range(3):
+                    block = spread[first : first + 16, 128 * c : 128 * c + 128]
+                    base[c, 8 * tr + y : 8 * tr + y + 1, 128 * half : 128 * half + 128] = jnp.sum(
+                        jnp.where(of_tile, block, 0.0), axis=0, keepdims=True
+                    )
+
+
 def denoise(
-    top, bottom, has_left, has_right, ext, x0, x1, e1, e2, d1, edge, w1, wb, wo, fo, out
+    top, bottom, has_left, has_right, ext, x0, x1, e1, e2, d1, edge, w1, wb, wo, fo, base, out
 ):
     tiles = ext[...].astype(BF16)
     lane = iota((256, 128), 1)
@@ -175,14 +189,18 @@
         n = rows_in * PITCH
         m = (rows_in - 2) * PITCH
         lane = iota((n, 128), 1)
-        edge[0:n, :] = jnp.where(
-            lane < 32,
-            ref[PAD + 1 : PAD + 1 + n, 0:128],
-            jnp.where(lane >= 96, ref[PAD - 1 : PAD - 1 + n, 128:256], 0.0),
-        )
+        beside = jnp.where(
+            lane < 64, ref[PAD + 1 : PAD + 1 + n, 0:128], ref[PAD - 1 : PAD - 1 + n, 128:256]
+        )
+        edge[0:n, :] = beside
+        outer = (iota((m, 128), 1) < 32) | (iota((m, 128), 1) >= 96)
+        between = pltpu.roll(beside, 64, 1)[PITCH : PITCH + m, :]
         wide = jnp.concatenate(
             [ref[PAD + PITCH * dy : PAD + PITCH * dy + m, :].astype(BF16) for dy in range(3)]
-            + [edge[PITCH * dy : PITCH * dy + m, :].astype(BF16) for dy in range(3)],
+            + [
+                jnp.where(outer, edge[0:m, :], between).astype(BF16),
+                edge[2 * PITCH : 2 * PITCH + m, :].astype(BF16),
+            ],
             axis=1,
         )
         return mm(wide, wb[layer])
@@ -191,11 +209,9 @@
     finish(d1, convolve(e2, 1, 20), 1)
     m = 16 * PITCH
     d2 = jnp.maximum(convolve(d1, 2, 18) + e1[PAD + 3 * PITCH : PAD + 3 * PITCH + m, :], 0.0)
-    last = jnp.concatenate(
-        [d2.astype(BF16), x0[PAD + 4 * PITCH : PAD + 4 * PITCH + m, :].astype(BF16)], axis=1
-    )
+    projected = mm(d2.astype(BF16), wo[...])
     for c in range(3):
-        fo[c] = mm(last, wo[:, 128 * c : 128 * c + 128])
+        fo[c] = projected[:, 128 * c : 128 * c + 128]
     of_group = iota((16, 128), 1) // 8
     for c in range(3):
         for half in range(2):
@@ -203,7 +219,8 @@
             for g in range(16):
                 rows = pl.ds(1 + 16 * half + g, 16, stride=PITCH)
                 found = jnp.where(of_group == g, fo[c, rows, :], found)
-            out[c, :, 128 * half : 128 * half + 128] = found.astype(BF16)
+            there = slice(128 * half, 128 * half + 128)
+            out[c, :, there] = (found + base[c, :, there]).astype(BF16)
 
 
 def kernel(
@@ -265,6 +282,7 @@
     wb,
     wo,
     fo,
+    base,
     am_send,
     am_recv,
     a_send,
@@ -504,6 +522,7 @@
     has_right = jnp.where(t < n_tile - 1, 1.0, 0.0)
     ext[PITCH + 1 : PITCH + 33, :] = own[0:32, :]
     ext[2 * PITCH + 1 : 2 * PITCH + 33, :] = own[32:64, :]
+    lay_out(composite, base)
     for copy in h_copies:
         copy.wait_recv()
     ext[1:33, :] = h_rows[0].astype(F32) * has_up
@@ -522,7 +541,7 @@
             ext[at : at + 1, :] = block[r : r + 1, :]
 
     denoise(
-        s == 0, s == n_slab - 1, has_left, has_right, ext, x0, x1, e1, e2, d1, edge, w1, wb, wo, fo, out
+        s == 0, s == n_slab - 1, has_left, has_right, ext, x0, x1, e1, e2, d1, edge, w1, wb, wo, fo, base, out
     )
 
     for copy in [*am_copies.values(), *a_copies.values()] + bm_copies + b_copies + h_copies:
@@ -595,9 +614,10 @@
             pltpu.VMEM((18 * PITCH + 2 * PAD, 256), F32),
             pltpu.VMEM((22 * PITCH, 128), F32),
             pltpu.VMEM((384, 256), BF16),
-            pltpu.VMEM((3, 1152, 256), BF16),
-            pltpu.VMEM((384, 384), BF16),
+            pltpu.VMEM((3, 1024, 256), BF16),
+            pltpu.VMEM((256, 384), BF16),
             pltpu.VMEM((3, 16 * PITCH, 128), F32),
+            pltpu.VMEM((3, 16, 256), F32),
             dma((n_tile,)),
             dma((n_tile,)),
             dma((n_tile,)),

time: 48.6 us -> 47.6 us (0.979)
  Pallas kernels: 47.1 us -> 46 us
    pallas_call x1, Pallas kernels: 47.1 us -> 46 us  [shards(): pl.pallas_call(functools.partial(kernel, n_slab, n_tile), out_shape=jax.S...]
where the time goes in v4:
time: 47.6 us; the launch traced here: 47.4 us
  Pallas kernels  46 us (97%)
  local copies, waits for them, and re-layouts  1.35 us (3%)
    pallas_call x1, Pallas kernels, shards(): pl.pallas_call(functools.partial(kernel, n_slab, n_tile), out_shape=jax.S...  46 us
    unnamed x1, local copies, waits for them, and re-layouts  1.35 us

profile of v4, /device:TPU:1, one launch (start us, length us, event | category | flops | bytes accessed | tf_op | source)
XLA Modules:
  0.0 47.4 jit_solution(6031647399626686408)
XLA Ops:
  0.0 46.0 %shard_map.109 = bf16[3,16,256]{2,1,0:T(8,128)(2,1)} custom-call(bf16[512,512]{1,0:T(8,128)(2,1)} %refs_0_.1, f32[3,512]{1,0:T(4,128)} %refs_1_.1, s32[1,512]{1,0:T(1,128)} %bitcast.19, s32[1,512]{1,0:T(1,128)} %bitcast.20, s32[1,512]{1,0:T(1,128)} %bitcast.21, s32[32,32]{1,0:T(8,128)} %refs_5_.1, bf16[9,4,32]{2,1,0:T(4,128)(2,1)} %bitcast.18, ...), custom_call_target="tpu_custom_call" | custom-call | tf_op jit(solution)/shard_map/pallas_call | solution.py:583
  46.0 1.3 %copy.13 = bf16[3,16,256]{2,1,0:T(8,128)(2,1)} copy(bf16[3,16,256]{2,1,0:T(8,128)(2,1)} %shard_map.109) | data formatting | bytes 49152

commit v5 on v4

--- a/solution.py
+++ b/solution.py
@@ -211,7 +211,7 @@
     d2 = jnp.maximum(convolve(d1, 2, 18) + e1[PAD + 3 * PITCH : PAD + 3 * PITCH + m, :], 0.0)
     projected = mm(d2.astype(BF16), wo[...])
     for c in range(3):
-        fo[c] = projected[:, 128 * c : 128 * c + 128]
+        fo[c, 0:m, :] = projected[:, 128 * c : 128 * c + 128]
     of_group = iota((16, 128), 1) // 8
     for c in range(3):
         for half in range(2):
@@ -311,9 +311,9 @@
 
     corners = [near(-1, -1), near(-1, 1), near(1, -1), near(1, 1)]
     greeted = (
-        [tile_peer(i) for i in range(1, n_tile)]
+        corners
         + [slab_peer(j) for j in range(1, n_slab)]
-        + corners
+        + [tile_peer(i) for i in range(1, n_tile)]
     )
     barrier = pltpu.get_barrier_semaphore()
     for peer in greeted:
@@ -616,7 +616,7 @@
             pltpu.VMEM((384, 256), BF16),
             pltpu.VMEM((3, 1024, 256), BF16),
             pltpu.VMEM((256, 384), BF16),
-            pltpu.VMEM((3, 16 * PITCH, 128), F32),
+            pltpu.VMEM((3, 17 * PITCH, 128), F32),
             pltpu.VMEM((3, 16, 256), F32),
             dma((n_tile,)),
             dma((n_tile,)),

time: 47.6 us -> 47.8 us (level)
  no operation moved by 1% of the time
where the time goes in v5:
time: 47.8 us; the launch traced here: 47.7 us
  Pallas kernels  46.3 us (97%)
  local copies, waits for them, and re-layouts  1.35 us (3%)
    pallas_call x1, Pallas kernels, shards(): pl.pallas_call(functools.partial(kernel, n_slab, n_tile), out_shape=jax.S...  46.3 us
    unnamed x1, local copies, waits for them, and re-layouts  1.35 us

profile of v5, /device:TPU:1, one launch (start us, length us, event | category | flops | bytes accessed | tf_op | source)
XLA Modules:
  0.0 47.7 jit_solution(12107031548182772428)
XLA Ops:
  0.0 46.3 %shard_map.109 = bf16[3,16,256]{2,1,0:T(8,128)(2,1)} custom-call(bf16[512,512]{1,0:T(8,128)(2,1)} %refs_0_.1, f32[3,512]{1,0:T(4,128)} %refs_1_.1, s32[1,512]{1,0:T(1,128)} %bitcast.19, s32[1,512]{1,0:T(1,128)} %bitcast.20, s32[1,512]{1,0:T(1,128)} %bitcast.21, s32[32,32]{1,0:T(8,128)} %refs_5_.1, bf16[9,4,32]{2,1,0:T(4,128)(2,1)} %bitcast.18, ...), custom_call_target="tpu_custom_call" | custom-call | tf_op jit(solution)/shard_map/pallas_call | solution.py:583
  46.3 1.3 %copy.13 = bf16[3,16,256]{2,1,0:T(8,128)(2,1)} copy(bf16[3,16,256]{2,1,0:T(8,128)(2,1)} %shard_map.109) | data formatting | bytes 49152
